TPU v7x, 128 devices: a whole 4x4x4 slice. The times are simulated.
128 devices in a mesh: row: 8 (over z_lo, x), col: 16 (over y, z_hi, core).
Axes of the slice: x: 4, y: 4, z: 4 (z_hi: 2, z_lo: 2; z = z_hi * 2 + z_lo), core: 2. Of those that a mesh axis runs over, the one named last changes fastest.
Arguments:
- inputs: bfloat16 [1024, 12288], P('row', 'col'), may hold values from -6 to 6
- pre_act: bfloat16 [1024, 24576], P('col', 'row'), may hold values from -6 to 6
- w_first: bfloat16 [12288, 24576], P('col', 'row'), may hold values from -0.0546875 to 0.0546875
- w_second: bfloat16 [24576, 12288], P('row', 'col'), may hold values from -0.0390625 to 0.0390625
- out_grad: bfloat16 [1024, 12288], P('row', 'col'), may hold values from -1.0546875 to 1.0546875
Outputs:
- input_grad: bfloat16 [1024, 12288], P('row', 'col')
- first_grad: bfloat16 [12288, 24576], P('col', 'row')
- second_grad: bfloat16 [24576, 12288], P('row', 'col')
All inputs are finite; a program needn't handle non-finite values.
Results may differ from a plain program's by a relative error of at most 0.025.
Values may be sent and summed in bfloat16 or wider, within the bound.
A program may use at most 128 MiB of HBM per device.

v0:
```python
import jax
import jax.numpy as jnp
from jax import lax
from jax.sharding import PartitionSpec as P


def gelu_back(pre32, grad32):
    values, pullback = jax.vjp(lambda v: jax.nn.gelu(v, approximate=True), pre32)
    return (values, pullback(grad32)[0])


def contract_rows(left, right):
    return lax.dot_general(
        left, right, (((0,), (0,)), ((), ())), preferred_element_type=jnp.float32
    )


def times_transposed(left, right):
    return lax.dot_general(
        left, right, (((1,), (1,)), ((), ())), preferred_element_type=jnp.float32
    )


def local(inputs, pre_act, w_first, w_second, out_grad):
    inputs_all, grad_all = (
        lax.all_gather(inputs, "row", axis=0, tiled=True),
        lax.all_gather(out_grad, "row", axis=0, tiled=True),
    )
    hidden_grad = lax.psum_scatter(
        times_transposed(grad_all, w_second).astype(jnp.bfloat16),
        "col",
        scatter_dimension=0,
        tiled=True,
    )
    values, slope = gelu_back(pre_act.astype(jnp.float32), hidden_grad.astype(jnp.float32))
    activated = values.astype(jnp.bfloat16)
    pre_grad = slope.astype(jnp.bfloat16)
    act_piece = lax.all_gather(activated, "col", axis=0, tiled=True)
    grad_piece = lax.all_gather(pre_grad, "col", axis=0, tiled=True)
    second_sum = contract_rows(act_piece, grad_all)
    first_sum = contract_rows(inputs_all, grad_piece)
    new_rows = times_transposed(grad_piece, w_first)
    input_part = new_rows
    second_sum, first_sum, input_part = (second_sum, first_sum, input_part)
    input_grad = lax.psum_scatter(
        input_part.astype(jnp.bfloat16), "row", scatter_dimension=0, tiled=True
    )
    return (input_grad, first_sum.astype(jnp.bfloat16), second_sum.astype(jnp.bfloat16))


def solution(mesh):
    placed = (P("row", "col"), P("col", "row"), P("col", "row"), P("row", "col"), P("row", "col"))
    return jax.shard_map(
        local,
        mesh=mesh,
        in_specs=placed,
        out_specs=(P("row", "col"), P("col", "row"), P("row", "col")),
        check_vma=False,
    )
```

profile of v0, /device:TPU:1, one launch (start us, length us, event | category | flops | bytes accessed | tf_op | source)
XLA Modules:
  0.0 367.5 jit_solution(4932044225269479181)
XLA Ops:
  7.2 0.0 all-gather.5.cloned.1.call-start
  7.2 0.7 all-gather.5.cloned.1.call-update
  7.9 0.0 reduce-scatter.3.cloned.1.call-start
  7.9 39.3 %all-gather.5.cloned.1.call-done = bf16[1024,768]{1,0:T(8,128)(2,1)} async-done(((bf16[128,768]{1,0:T(8,128)(2,1)}), bf16[1024,768]{1,0:T(8,128)(2,1)}) %all-gather.5.cloned.1.call-update) | async-done | bytes 1572880 | tf_op jit(solution)/shard_map/all_gather | solution.py:27
  47.3 9.2 %convolution_convert_fusion = bf16[1024,3072]{1,0:T(8,128)(2,1)} fusion(bf16[1024,768]{1,0:T(8,128)(2,1)} %all-gather.5.cloned.1.call-done, bf16[3072,768]{1,0:T(8,128)(2,1)} %param.8), kind=kOutput, calls=%fused_computation | convolution fusion | flops 4834983936 | bytes 12582912 | tf_op jit(solution)/shard_map/dot_general | solution.py:19
  56.5 0.0 copy-start
  56.5 0.0 reduce-scatter.3.cloned.1.call-update
  56.6 0.0 all-gather.7.cloned.1.call-start
  56.6 93.9 %reduce-scatter.3.cloned.1.call-done = bf16[64,3072]{1,0:T(8,128)(2,1)} async-done(((bf16[1024,3072]{1,0:T(8,128)(2,1)}), bf16[64,3072]{1,0:T(8,128)(2,1)}) %reduce-scatter.3.cloned.1.call-update) | async-done | bytes 393232 | tf_op jit(solution)/shard_map/reduce_scatter | solution.py:29
  150.5 0.0 copy-done
  150.5 2.5 fusion.11
  153.0 0.0 all-gather.7.cloned.1.call-update
  153.0 0.0 all-gather.9.cloned.1.call-start
  153.1 0.5 all-gather.9.cloned.1.call-update
  153.6 0.0 all-gather.11.cloned.1.call-start
  153.7 0.5 all-gather.11.cloned.1.call-update
  154.2 0.0 reduce-scatter.5.cloned.1.call-start
  154.3 63.9 %all-gather.7.cloned.1.call-done = bf16[1024,3072]{1,0:T(8,128)(2,1)} async-done(((bf16[64,3072]{1,0:T(8,128)(2,1)}), bf16[1024,3072]{1,0:T(8,128)(2,1)}) %all-gather.7.cloned.1.call-update) | async-done | bytes 6291472 | tf_op jit(solution)/shard_map/all_gather | solution.py:39
  218.1 9.5 %convolution_convert_fusion.3 = bf16[1024,768]{1,0:T(8,128)(2,1)} fusion(bf16[1024,3072]{1,0:T(8,128)(2,1)} %all-gather.7.cloned.1.call-done, bf16[768,3072]{1,0:T(8,128)(2,1)} %param.7), kind=kOutput, calls=%fused_computation.4 | convolution fusion | flops 4832624640 | bytes 12582912 | tf_op jit(solution)/shard_map/dot_general | solution.py:19
  227.6 0.0 reduce-scatter.5.cloned.1.call-update
  227.6 24.2 %all-gather.9.cloned.1.call-done = bf16[1024,768]{1,0:T(8,128)(2,1)} async-done(((bf16[128,768]{1,0:T(8,128)(2,1)}), bf16[1024,768]{1,0:T(8,128)(2,1)}) %all-gather.9.cloned.1.call-update) | async-done | bytes 1572880 | tf_op jit(solution)/shard_map/all_gather | solution.py:26
  251.8 9.1 %fusion = bf16[768,3072]{0,1:T(8,128)(2,1)} fusion(bf16[1024,3072]{1,0:T(8,128)(2,1)} %all-gather.7.cloned.1.call-done, bf16[1024,768]{1,0:T(8,128)(2,1)} %all-gather.9.cloned.1.call-done), kind=kOutput, calls=%fused_computation.3 | convolution fusion | flops 4834197504 | bytes 12582912 | tf_op jit(solution)/shard_map/dot_general | solution.py:13
  260.9 0.0 copy-start.1
  260.9 6.7 %copy.8 = bf16[768,3072]{1,0:T(8,128)(2,1)} copy(bf16[768,3072]{0,1:T(8,128)(2,1)} %fusion) | data formatting | bytes 9437184
  267.7 56.5 %all-gather.11.cloned.1.call-done = bf16[1024,3072]{1,0:T(8,128)(2,1)} async-done(((bf16[64,3072]{1,0:T(8,128)(2,1)}), bf16[1024,3072]{1,0:T(8,128)(2,1)}) %all-gather.11.cloned.1.call-update) | async-done | bytes 6291472 | tf_op jit(solution)/shard_map/all_gather | solution.py:38
  324.2 0.0 copy-done.1
  324.2 9.7 %convolution_convert_fusion.1 = bf16[3072,768]{1,0:T(8,128)(2,1)} fusion(bf16[1024,3072]{1,0:T(8,128)(2,1)} %all-gather.11.cloned.1.call-done, bf16[1024,768]{1,0:T(8,128)(2,1)S(1)} %copy-done.1), kind=kOutput, calls=%fused_computation.1 | convolution fusion | flops 4834197504 | bytes 12582912 | tf_op jit(solution)/shard_map/dot_general | solution.py:13
  333.8 26.8 %reduce-scatter.5.cloned.1.call-done = bf16[128,768]{1,0:T(8,128)(2,1)} async-done(((bf16[1024,768]{1,0:T(8,128)(2,1)}), bf16[128,768]{1,0:T(8,128)(2,1)}) %reduce-scatter.5.cloned.1.call-update) | async-done | bytes 196624 | tf_op jit(solution)/shard_map/reduce_scatter | solution.py:45
Async XLA Ops:
  7.2 40.1 %all-gather.5.cloned.1.call-start = ((), (), s32[]{:S(2)}) async-start(), calls=%async_computation.2 | async-start | bytes 1769472 | tf_op jit(solution)/shard_map/all_gather | solution.py:27
  7.9 142.6 %reduce-scatter.3.cloned.1.call-start = ((), (), s32[]{:S(2)}) async-start(), calls=%async_computation.3 | async-start | bytes 6684672 | tf_op jit(solution)/shard_map/reduce_scatter | solution.py:29
  56.5 94.0 %copy-start = (bf16[64,3072]{1,0:T(8,128)(2,1)S(1)}, bf16[64,3072]{1,0:T(8,128)(2,1)}, u32[]{:S(2)}) copy-start(bf16[64,3072]{1,0:T(8,128)(2,1)} %param.6) | copy-start | bytes 1179652
  56.6 161.6 %all-gather.7.cloned.1.call-start = ((), (), s32[]{:S(2)}) async-start(), calls=%async_computation.4 | async-start | bytes 6684672 | tf_op jit(solution)/shard_map/all_gather | solution.py:39
  153.0 98.8 %all-gather.9.cloned.1.call-start = ((), (), s32[]{:S(2)}) async-start(), calls=%async_computation.6 | async-start | bytes 1769472 | tf_op jit(solution)/shard_map/all_gather | solution.py:26
  153.6 170.5 %all-gather.11.cloned.1.call-start = ((), (), s32[]{:S(2)}) async-start(), calls=%async_computation.7 | async-start | bytes 6684672 | tf_op jit(solution)/shard_map/all_gather | solution.py:38
  154.2 206.4 %reduce-scatter.5.cloned.1.call-start = ((), (), s32[]{:S(2)}) async-start(), calls=%async_computation.5 | async-start | bytes 1769472 | tf_op jit(solution)/shard_map/reduce_scatter | solution.py:45
  260.9 63.2 %copy-start.1 = (bf16[1024,768]{1,0:T(8,128)(2,1)S(1)}, bf16[1024,768]{1,0:T(8,128)(2,1)}, u32[]{:S(2)}) copy-start(bf16[1024,768]{1,0:T(8,128)(2,1)} %all-gather.5.cloned.1.call-done) | copy-start | bytes 4718596
Sparse Core Ops, SparseCore 0:
  9.6 37.6 all-gather.4
  56.7 93.8 reduce-scatter.2
  153.5 64.5 all-gather.6
  219.6 32.1 all-gather.8
  254.1 70.0 all-gather.10
  327.0 33.6 reduce-scatter.4
where the time goes:
time: 372 us; the launch traced here: 368 us
  waiting for transfers between devices  306 us (82%)
  matrix products  37.5 us (10%)
  between operations  14.1 us (4%)
  local copies, waits for them, and re-layouts  6.74 us (2%)
    reduce_scatter x1, waiting for transfers between devices, local(): lax.psum_scatter(times_transposed(grad_all, w_second).astype(jnp.bfloat16...  93.9 us
    all_gather x1, waiting for transfers between devices, local(): grad_piece = lax.all_gather(pre_grad, 'col', axis=0, tiled=True)  63.9 us
    all_gather x1, waiting for transfers between devices, local(): act_piece = lax.all_gather(activated, 'col', axis=0, tiled=True)  56.5 us
    all_gather x1, waiting for transfers between devices, local(): lax.all_gather(out_grad, 'row', axis=0, tiled=True)  39.3 us
    reduce_scatter x1, waiting for transfers between devices, local(): lax.psum_scatter(input_part.astype(jnp.bfloat16), 'row', scatter_dimensio...  26.8 us
    all_gather x1, waiting for transfers between devices, local(): lax.all_gather(inputs, 'row', axis=0, tiled=True)  24.2 us
    dot_general x2, matrix products, contract_rows(): lax.dot_general(left, right, (((0,), (0,)), ((), ())), preferred_element_...  18.8 us
    dot_general x2, matrix products, times_transposed(): lax.dot_general(left, right, (((1,), (1,)), ((), ())), preferred_element_...  18.7 us
  transfers between devices with their start and end apart: 6, of which 6 were waited for; matrix products, arithmetic and copies ran while one was open for 10% of the time, Pallas kernels for 0%

commit v1 on v0

v1 whole, which is shorter than its diff:
```python
import jax
import jax.numpy as jnp
from jax import lax
from jax.experimental import pallas as pl
from jax.experimental.pallas import tpu as pltpu
from jax.sharding import PartitionSpec as P

MESH = pl.DeviceIdType.MESH
T = 128
W = 768
BF = jnp.bfloat16
F32 = jnp.float32
ROOT = 0.7978845608028654
CUBE = 0.044715


def rows(block):
    return pl.ds(pl.multiple_of(block * T, T), T)


def rt_dot(left, right):
    return lax.dot_general(left, right, (((1,), (1,)), ((), ())), preferred_element_type=F32)


def tl_dot(left, right):
    return lax.dot_general(left, right, (((0,), (0,)), ((), ())), preferred_element_type=F32)


class Group:
    def __init__(self, g, h, device, block):
        self.g, self.h = g, h
        self.above, self.below, self.pair = device((g + 1) % 4, h), device((g + 3) % 4, h), device(g, 1 - h)
        self.block = lambda dg, other: block((g + dg) % 4, (1 - h) if other else h)


class Gather:
    OWNER = ((0, True), (3, False), (1, False), (3, True), (1, True), (2, False), (2, True))

    def __init__(self, group, buf, mate_buf, mate, ssem, rsem, own_src=None):
        self.group, self.buf, self.mate_buf, self.mate = group, buf, mate_buf, mate
        self.ssem, self.rsem, self.own_src = ssem, rsem, own_src
        self.sent = []

    def _copy(self, slot, owner, device, src=None):
        at = rows(self.group.block(*owner))
        return pltpu.make_async_remote_copy(
            self.buf.at[at] if src is None else src, self.buf.at[at],
            self.ssem.at[slot], self.rsem.at[slot], device, MESH)

    def _send(self, slot, owner, device, src=None):
        c = self._copy(slot, owner, device, src)
        c.start()
        self.sent.append(c)

    def _mate(self, index, owner, src=None):
        if self.mate is None:
            return
        at = rows(self.group.block(*owner))
        c = pltpu.make_async_remote_copy(
            self.buf.at[at] if src is None else src, self.buf.at[at],
            self.ssem.at[7 + index], self.rsem.at[7 + index], self.mate, MESH)
        c.start()
        self.sent.append(c)

    def start(self):
        g, own = self.group, (0, False)
        self._send(0, own, g.pair, self.own_src)
        self._send(1, own, g.above, self.own_src)
        self._send(2, own, g.below, self.own_src)
        self._mate(7, own, self.own_src)

    def take(self, slot):
        g, owner = self.group, self.OWNER[slot]
        self._copy(slot, owner, g.pair).wait_recv()
        if slot == 0:
            self._send(3, owner, g.above)
            self._send(4, owner, g.below)
        elif slot == 1:
            self._send(5, owner, g.above)
        elif slot == 4:
            self._send(6, owner, g.below)
        self._mate(slot, owner)

    def take_mate(self):
        for index, owner in enumerate(self.OWNER + ((0, False),)):
            at = rows(self.group.block(*owner))
            pltpu.make_async_remote_copy(
                self.mate_buf.at[at], self.mate_buf.at[at],
                self.ssem.at[7 + index], self.rsem.at[7 + index], self.mate, MESH).wait_recv()

    def drain(self):
        for c in self.sent:
            c.wait_send()


class Scatter:
    def __init__(self, group, part, rbuf, ssem, rsem):
        self.group, self.part, self.rbuf, self.ssem, self.rsem = group, part, rbuf, ssem, rsem
        self.sent = []

    def at(self, dg, other):
        return rows(self.group.block(dg, other))

    def _copy(self, slot, at, device):
        return pltpu.make_async_remote_copy(
            self.part.at[at], self.rbuf.at[slot], self.ssem.at[slot], self.rsem.at[slot], device, MESH)

    def _send(self, slot, dg, other, device):
        c = self._copy(slot, self.at(dg, other), device)
        c.start()
        self.sent.append(c)

    def _wait(self, slot):
        self._copy(slot, self.at(0, False), self.group.pair).wait_recv()

    def far(self):
        self._send(0, 2, False, self.group.above)
        self._send(1, 2, True, self.group.below)

    def near(self):
        self._send(2, 1, True, self.group.above)
        self._send(3, 3, False, self.group.below)

    def fold(self):
        for slot, dg, other, device in ((0, 1, False, self.group.above), (1, 3, True, self.group.below)):
            self._wait(slot)
            at = self.at(dg, other)
            self.part[at] = (self.part[at].astype(F32) + self.rbuf[slot].astype(F32)).astype(BF)
            self._send(slot + 4, dg, other, device)

    def _total(self, other):
        direct, folded = (2, 5) if other else (3, 4)
        return (self.part[self.at(0, other)].astype(F32) + self.rbuf[direct].astype(F32)
                + self.rbuf[folded].astype(F32))

    def cross(self):
        self._wait(2)
        self._wait(5)
        self.part[self.at(0, True)] = self._total(True).astype(BF)
        self._send(6, 0, True, self.group.pair)

    def result(self):
        self._wait(3)
        self._wait(4)
        own = self._total(False)
        self._wait(6)
        return own + self.rbuf[6].astype(F32)

    def drain(self):
        for c in self.sent:
            c.wait_send()


def kernel(in_ref, pre_ref, w1_ref, w2_ref, og_ref, dx_ref, dw1_ref, dw2_ref,
           og_all, in_all, act_all, pre_all, pre_loc, slope, w1, w2, part, inp, acc, rbuf, out1, out2, dxv,
           g_ss, g_rs, r_ss, r_rs, k_ss, k_rs, l_sem, o_sem):
    r, c = lax.axis_index("row"), lax.axis_index("col")
    x, zl = r % 4, r // 4
    y, zh, k = c // 4, (c // 2) % 2, c % 2
    half = W * 2
    mate = (r, c + 1 - 2 * k)
    by_row = Group(x, zl, lambda g, h: (h * 4 + g, c), lambda g, h: h * 4 + g)
    by_col = Group(y, zh, lambda g, h: (r, g * 4 + h * 2 + k), lambda g, h: g * 2 + h)

    def cols(core, s):
        return pl.ds(pl.multiple_of(core * half + s * W, W), W)

    own64 = pl.ds(pl.multiple_of(k * 64, 64), 64)
    w2_rows = pl.ds(pl.multiple_of(k * half, half), half)
    w2_mate_rows = pl.ds(pl.multiple_of((1 - k) * half, half), half)
    loads = [
        pltpu.make_async_copy(pre_ref.at[:, cols(k, 0)], pre_loc.at[0, own64], l_sem.at[0]),
        pltpu.make_async_copy(pre_ref.at[:, cols(k, 1)], pre_loc.at[1, own64], l_sem.at[1]),
        pltpu.make_async_copy(og_ref, og_all.at[k, rows(r)], l_sem.at[2]),
        pltpu.make_async_copy(w2_ref.at[w2_rows], w2.at[k], l_sem.at[3]),
        pltpu.make_async_copy(in_ref, in_all.at[rows(r)], l_sem.at[4]),
        pltpu.make_async_copy(w1_ref, w1, l_sem.at[5]),
    ]
    for load in loads:
        load.start()

    barrier = pltpu.get_barrier_semaphore()
    friends = (mate, by_row.above, by_row.below, by_row.pair, by_col.above, by_col.below, by_col.pair)
    for friend in friends:
        pl.semaphore_signal(barrier, inc=1, device_id=friend, device_id_type=MESH)
    pl.semaphore_wait(barrier, len(friends))

    gathers = (
        Gather(by_row, og_all.at[k], og_all.at[1 - k], mate, g_ss.at[0], g_rs.at[0], og_ref),
        Gather(by_row, in_all, None, None, g_ss.at[1], g_rs.at[1], in_ref),
        Gather(by_col, act_all.at[2 * k], act_all.at[2 - 2 * k], mate, g_ss.at[2], g_rs.at[2]),
        Gather(by_col, act_all.at[2 * k + 1], act_all.at[3 - 2 * k], mate, g_ss.at[3], g_rs.at[3]),
        Gather(by_col, pre_all.at[2 * k], pre_all.at[2 - 2 * k], mate, g_ss.at[4], g_rs.at[4]),
        Gather(by_col, pre_all.at[2 * k + 1], pre_all.at[3 - 2 * k], mate, g_ss.at[5], g_rs.at[5]),
    )
    og, xs, act0, act1, pre0, pre1 = gathers
    hid = [Scatter(by_col, part.at[s], rbuf.at[s], r_ss.at[s], r_rs.at[s]) for s in range(2)]
    dx = Scatter(by_row, inp, rbuf.at[2], r_ss.at[2], r_rs.at[2])

    to_mate = [
        pltpu.make_async_remote_copy(pre_ref.at[:, cols(1 - k, 0)], pre_loc.at[0, own64], k_ss.at[0], k_rs.at[0], mate, MESH),
        pltpu.make_async_remote_copy(pre_ref.at[:, cols(1 - k, 1)], pre_loc.at[1, own64], k_ss.at[1], k_rs.at[1], mate, MESH),
        pltpu.make_async_remote_copy(w2_ref.at[w2_mate_rows], w2.at[k], k_ss.at[2], k_rs.at[2], mate, MESH),
    ]
    to_mate[0].start()
    to_mate[1].start()
    og.start()
    to_mate[2].start()

    def activate(s, gather):
        a = pre_loc[s].astype(F32)
        t = jnp.tanh(ROOT * (a + CUBE * (a * a * a)))
        act_all[2 * k + s, rows(by_col.block(0, False))] = (0.5 * a * (1.0 + t)).astype(BF)
        slope[s] = 0.5 * (1.0 + t) + 0.5 * a * (1.0 - t * t) * (ROOT * (1.0 + 3.0 * CUBE * (a * a)))

    def pre_grad(s):
        grad = hid[s].result().astype(BF).astype(F32)
        pre_all[2 * k + s, rows(by_col.block(0, False))] = (slope[s] * grad).astype(BF)

    def hidden(s, dg):
        at = pl.ds(pl.multiple_of(((y + dg) % 4) * 2 * T, 2 * T), 2 * T)

        def tile(n, _):
            units = pl.ds(pl.multiple_of(s * W + n * 256, 256), 256)
            to = pl.ds(pl.multiple_of(n * 256, 256), 256)
            part[s, at, to] = (rt_dot(og_all[0, at], w2[0, units]) + rt_dot(og_all[1, at], w2[1, units])).astype(BF)
            return 0

        lax.fori_loop(0, 3, tile, 0)

    def weight_grad(left, right, out, slot, dst):
        def tile(m, _):
            at = pl.ds(pl.multiple_of(m * 256, 256), 256)
            out[slot, at] = tl_dot(left[:, at], right[...]).astype(BF)
            return 0

        lax.fori_loop(0, 3, tile, 0)
        copy = pltpu.make_async_copy(out.at[slot], dst[0], dst[1])
        copy.start()
        return copy

    outs = []

    def second_grad(q):
        outs.append(weight_grad(act_all.at[q], og_all.at[k], out2, q, (dw2_ref.at[pl.ds(q * W, W)], o_sem.at[q])))

    def first_grad(q):
        outs.append(weight_grad(in_all, pre_all.at[q], out1, q, (dw1_ref.at[:, pl.ds(q * W, W)], o_sem.at[4 + q])))

    def input_early():
        def tile(m, _):
            at = pl.ds(pl.multiple_of(m * 256, 256), 256)
            acc[at] = (rt_dot(pre_all[0, at], w1[:, pl.ds(0, W)]) + rt_dot(pre_all[2, at], w1[:, pl.ds(2 * W, W)]))
            return 0

        lax.fori_loop(0, 4, tile, 0)

    def input_late(dg):
        for other in (False, True):
            at = rows(by_row.block(dg, other))

            def tile(n, _):
                to = pl.ds(pl.multiple_of(n * 256, 256), 256)
                inp[at, to] = (acc[at, to] + rt_dot(pre_all[1, at], w1[to, pl.ds(W, W)])
                               + rt_dot(pre_all[3, at], w1[to, pl.ds(3 * W, W)])).astype(BF)
                return 0

            lax.fori_loop(0, 3, tile, 0)

    loads[0].wait()
    to_mate[0].wait_recv()
    activate(0, act0)
    act0.start()
    loads[1].wait()
    to_mate[1].wait_recv()
    activate(1, act1)

    og.take(0)
    act0.take(0)
    for slot in (1, 2, 4, 3):
        og.take(slot)
        act0.take(slot)
    og.take(5)
    og.take(6)
    xs.start()
    loads[2].wait()
    loads[3].wait()
    to_mate[2].wait_recv()
    og.take_mate()

    hidden(0, 2)
    hid[0].far()
    hidden(0, 1)
    hidden(0, 3)
    hid[0].near()
    hidden(0, 0)
    act0.take(5)
    act0.take(6)
    hid[0].fold()
    hidden(1, 2)
    hid[1].far()
    hidden(1, 1)
    hidden(1, 3)
    hid[1].near()
    hidden(1, 0)
    xs.take(0)
    xs.take(1)
    xs.take(2)
    act0.take_mate()
    second_grad(0)
    hid[0].cross()
    hid[1].fold()
    xs.take(4)
    xs.take(3)
    second_grad(2)
    pre_grad(0)
    pre0.start()
    hid[1].cross()
    pre0.take(0)
    pre0.take(1)
    pre0.take(2)
    pre_grad(1)
    pre1.start()
    xs.take(5)
    xs.take(6)
    loads[4].wait()
    loads[5].wait()
    pre0.take(4)
    pre0.take(3)
    pre1.take(0)
    pre0.take(5)
    pre0.take(6)
    pre1.take(1)
    pre1.take(2)
    act1.start()
    pre0.take_mate()
    input_early()
    pre1.take(4)
    pre1.take(3)
    first_grad(0)
    act1.take(0)
    pre1.take(5)
    pre1.take(6)
    pre1.take_mate()

    input_late(2)
    dx.far()
    input_late(1)
    input_late(3)
    dx.near()
    input_late(0)
    act1.take(1)
    act1.take(2)
    first_grad(2)
    dx.fold()
    act1.take(4)
    act1.take(3)
    first_grad(1)
    dx.cross()
    act1.take(5)
    act1.take(6)
    first_grad(3)
    act1.take_mate()
    second_grad(1)
    second_grad(3)
    dxv[...] = dx.result().astype(BF)
    last = pltpu.make_async_copy(dxv, dx_ref, o_sem.at[8])
    last.start()
    for item in (*gathers, *hid, dx):
        item.drain()
    for copy in to_mate:
        copy.wait_send()
    for copy in outs:
        copy.wait()
    last.wait()


def local(inputs, pre_act, w_first, w_second, out_grad):
    sem = pltpu.SemaphoreType.DMA
    vm = lambda *shape, dtype=BF: pltpu.VMEM(shape, dtype)
    return pl.pallas_call(
        kernel,
        out_shape=(
            jax.ShapeDtypeStruct((T, W), BF),
            jax.ShapeDtypeStruct((W, 4 * W), BF),
            jax.ShapeDtypeStruct((4 * W, W), BF),
        ),
        in_specs=[pl.BlockSpec(memory_space=pl.ANY)] * 5,
        out_specs=[pl.BlockSpec(memory_space=pl.ANY)] * 3,
        scratch_shapes=[
            vm(2, 8 * T, W),
            vm(8 * T, W),
            vm(4, 8 * T, W),
            vm(4, 8 * T, W),
            vm(2, T, W),
            vm(2, T, W, dtype=F32),
            vm(W, 4 * W),
            vm(2, 2 * W, W),
            vm(2, 8 * T, W),
            vm(8 * T, W),
            vm(8 * T, W, dtype=F32),
            vm(3, 7, T, W),
            vm(4, W, W),
            vm(4, W, W),
            vm(T, W),
            sem((6, 15)), sem((6, 15)), sem((3, 7)), sem((3, 7)), sem((3,)), sem((3,)), sem((6,)), sem((9,)),
        ],
        compiler_params=pltpu.CompilerParams(
            collective_id=0, has_side_effects=True, vmem_limit_bytes=62 * 2**20
        ),
        cost_estimate=pl.CostEstimate(flops=19_327_352_832, bytes_accessed=20_000_000, transcendentals=400_000),
        name="ffn_back",
    )(inputs, pre_act, w_first, w_second, out_grad)


def solution(mesh):
    placed = (P("row", "col"), P("col", "row"), P("col", "row"), P("row", "col"), P("row", "col"))
    return jax.shard_map(
        local,
        mesh=mesh,
        in_specs=placed,
        out_specs=(P("row", "col"), P("col", "row"), P("row", "col")),
        check_vma=False,
    )
```

time: 372 us -> 123 us (0.33)
  waiting for transfers between devices: 306 us -> 0 us
  Pallas kernels: 0 us -> 112 us
  matrix products: 37.5 us -> 0 us
  between operations: 14.1 us -> 0.65 us
    all_gather x4 -> x0, waiting for transfers between devices: 184 us -> none  [the longest x1 63.9 us: local(): grad_piece = lax.all_gather(pre_grad, 'col', axis=0, tiled=True)]
    reduce_scatter x2 -> x0, waiting for transfers between devices: 121 us -> none  [the longest x1 93.9 us: local(): lax.psum_scatter(times_transposed(grad_all, w_second).astype(jnp.bfloat16...]
    pallas_call x0 -> x1, Pallas kernels: none -> 112 us  [local(): pl.pallas_call(kernel, out_shape=(jax.ShapeDtypeStruct((T, W), BF), jax.S...]
    dot_general x4 -> x0, matrix products: 37.5 us -> none  [the longest x2 18.8 us: contract_rows(): lax.dot_general(left, right, (((0,), (0,)), ((), ())), preferred_element_...]
    unnamed x5 -> x7, local copies, waits for them, and re-layouts: 6.74 us -> 8.86 us
  transfers between devices with their start and end apart: 6 -> 0, of which waited for: 6 -> 0; matrix products, arithmetic and copies ran while one was open for 10% -> 0% of each run, Pallas kernels for 0% -> 0%
where the time goes in v1:
time: 123 us; the launch traced here: 122 us
  Pallas kernels  112 us (91%)
  local copies, waits for them, and re-layouts  8.86 us (7%)
    pallas_call x1, Pallas kernels, local(): pl.pallas_call(kernel, out_shape=(jax.ShapeDtypeStruct((T, W), BF), jax.S...  112 us
    unnamed x7, local copies, waits for them, and re-layouts  8.86 us

profile of v1, /device:TPU:1, one launch (start us, length us, event | category | flops | bytes accessed | tf_op | source)
XLA Modules:
  0.0 122.0 jit_solution(13079478491154666151)
XLA Ops:
  0.6 112.5 %ffn_back.1 = (bf16[128,768]{1,0:T(8,128)(2,1)}, bf16[768,3072]{1,0:T(8,128)(2,1)}, bf16[3072,768]{1,0:T(8,128)(2,1)}) custom-call(bf16[128,768]{1,0:T(8,128)(2,1)} %in_ref.1, bf16[64,3072]{1,0:T(8,128)(2,1)} %pre_ref.1, bf16[768,3072]{1,0:T(8,128)(2,1)} %w1_ref.1, bf16[3072,768]{1,0:T(8,128)(2,1)} %w2_ref.1, bf16[128,768]{1,0:T(8,128)(2,1)} %og_ref.1), custom_call_target="tpu_custom_call" | custom-call | flops 19327352832 | bytes 20000000 | tf_op jit(solution)/shard_map/ffn_back/pallas_call | solution.py:381
  113.1 0.0 slice-start
  113.1 1.8 %copy.11 = bf16[128,768]{1,0:T(8,128)(2,1)} copy(bf16[128,768]{1,0:T(8,128)(2,1)} %get-tuple-element.6) | data formatting | bytes 393216
  114.9 0.0 slice-start.1
  114.9 4.9 %copy.12 = bf16[768,3072]{1,0:T(8,128)(2,1)} copy(bf16[768,3072]{1,0:T(8,128)(2,1)} %get-tuple-element.7) | data formatting | bytes 9437184
  119.8 0.0 slice-done
  119.8 0.0 slice-done.1
  119.8 2.2 %copy.13 = bf16[3072,768]{1,0:T(8,128)(2,1)} copy(bf16[3072,768]{1,0:T(8,128)(2,1)S(1)} %bitcast.1) | data formatting | bytes 9437184
  (1 shorter events, 0.0 us)
Async XLA Ops:
  113.1 6.7 %slice-start = ((s8[4718592]{0:T(1024)(128)(4,1)}), s8[4194304]{0:T(1024)(128)(4,1)S(1)}, s32[]{:S(2)}) async-start(s8[4718592]{0:T(1024)(128)(4,1)} %bitcast), calls=%async_computation | async-start | bytes 8388608
  114.9 4.9 %slice-start.1 = ((s8[4718592]{0:T(1024)(128)(4,1)}), s8[524288]{0:T(1024)(128)(4,1)S(1)}, s32[]{:S(2)}) async-start(s8[4718592]{0:T(1024)(128)(4,1)} %bitcast), calls=%async_computation.1 | async-start | bytes 1048576

commit v2 on v0

v2 whole, which is shorter than its diff:
```python
import jax
import jax.numpy as jnp
from jax import lax
from jax.experimental import pallas as pl
from jax.experimental.pallas import tpu as pltpu
from jax.sharding import PartitionSpec as P

MESH = pl.DeviceIdType.MESH
T = 64
HALF = 512
W = 768
U = 1536
BF = jnp.bfloat16
F32 = jnp.float32
ROOT = 0.7978845608028654
CUBE = 0.044715


def dot(left, right):
    return jnp.dot(left, right, preferred_element_type=F32)


def tl_dot(left, right):
    return lax.dot_general(left, right, (((0,), (0,)), ((), ())), preferred_element_type=F32)


class Group:
    def __init__(self, g, h, device, block):
        self.g, self.h = g, h
        self.above, self.below, self.pair = device((g + 1) % 4, h), device((g + 3) % 4, h), device(g, 1 - h)
        self.block = lambda dg, other: block((g + dg) % 4, (1 - h) if other else h)


class Gather:
    def __init__(self, group, buf, mate_buf, mate, ssem, rsem, own_src=None):
        self.group, self.buf, self.mate_buf, self.mate = group, buf, mate_buf, mate
        self.ssem, self.rsem, self.own_src = ssem, rsem, own_src
        self.sent = []

    def _ref(self, buf, owner, part=None):
        at = pl.ds(pl.multiple_of(self.group.block(*owner) * T, T), T)
        if len(buf.shape) == 2:
            return buf.at[at]
        return buf.at[:, at] if part is None else buf.at[part, at]

    def _copy(self, slot, owner, device, part=None):
        ref = self._ref(self.buf, owner, part)
        own = owner == (0, False) and self.own_src is not None
        return pltpu.make_async_remote_copy(
            self.own_src if own else ref, ref, self.ssem.at[slot], self.rsem.at[slot], device, MESH)

    def _send(self, slot, owner, device, part=None):
        c = self._copy(slot, owner, device, part)
        c.start()
        self.sent.append(c)

    def _mate(self, owner):
        if self.mate is not None:
            self._send(8 + owner[0] * 2 + int(owner[1]), owner, self.mate)

    def take_mate(self):
        for dg in range(4):
            for other in (False, True):
                ref, slot = self._ref(self.mate_buf, (dg, other)), 8 + dg * 2 + int(other)
                pltpu.make_async_remote_copy(
                    ref, ref, self.ssem.at[slot], self.rsem.at[slot], self.mate, MESH).wait_recv()

    def drain(self):
        for c in self.sent:
            c.wait_send()


class PairFirst(Gather):
    OWNER = ((0, True), (3, False), (1, False), (3, True), (1, True), (2, False), (2, True))

    def start(self):
        g, own = self.group, (0, False)
        self._send(0, own, g.pair)
        self._send(1, own, g.above)
        self._send(2, own, g.below)
        self._mate(own)

    def take(self, *slots):
        g = self.group
        for slot in slots:
            owner = self.OWNER[slot]
            self._copy(slot, (owner[0], owner[1]), g.pair).wait_recv()
            if slot == 0:
                self._send(3, owner, g.above)
                self._send(4, owner, g.below)
            elif slot == 1:
                self._send(5, owner, g.above)
            elif slot == 4:
                self._send(6, owner, g.below)
            self._mate(owner)


class RingFirst(Gather):
    def start(self):
        g, own = self.group, (0, False)
        self._send(0, own, g.above)
        self._send(1, own, g.below)
        self._mate(own)

    def give_own(self):
        self._send(4, (0, False), self.group.pair)

    def take_near(self):
        g = self.group
        for slot, dg, on, part in ((0, 3, g.above, 0), (1, 1, g.below, 1)):
            owner = (dg, False)
            self._copy(slot, owner, g.pair).wait_recv()
            self._send(2 + part, owner, on, part)
            self._mate(owner)

    def give_near(self):
        self._send(5, (3, False), self.group.pair)
        self._send(6, (1, False), self.group.pair)

    def take_far(self):
        g, owner = self.group, (2, False)
        for part in (0, 1):
            self._copy(2 + part, owner, g.pair, part).wait_recv()
        self._mate(owner)

    def give_far(self):
        self._send(7, (2, False), self.group.pair)

    def take_pair(self, *places):
        for place in places:
            owner = ((0, 3, 1, 2)[place], True)
            self._copy(4 + place, owner, self.group.pair).wait_recv()
            self._mate(owner)


class Scatter:
    def __init__(self, group, part, rbuf, ssem, rsem):
        self.group, self.part, self.rbuf, self.ssem, self.rsem = group, part, rbuf, ssem, rsem
        self.sent = []

    def at(self, dg, other):
        return pl.ds(pl.multiple_of(self.group.block(dg, other) * T, T), T)

    def _copy(self, slot, at, device):
        return pltpu.make_async_remote_copy(
            self.part.at[at], self.rbuf.at[slot], self.ssem.at[slot], self.rsem.at[slot], device, MESH)

    def _send(self, slot, dg, other, device):
        c = self._copy(slot, self.at(dg, other), device)
        c.start()
        self.sent.append(c)

    def _wait(self, slot):
        self._copy(slot, self.at(0, False), self.group.pair).wait_recv()

    def far(self):
        self._send(0, 2, False, self.group.above)
        self._send(1, 2, True, self.group.below)

    def near(self):
        self._send(2, 1, True, self.group.above)
        self._send(3, 3, False, self.group.below)

    def fold(self):
        for slot, dg, other, device in ((0, 1, False, self.group.above), (1, 3, True, self.group.below)):
            self._wait(slot)
            at = self.at(dg, other)
            self.part[at] = (self.part[at].astype(F32) + self.rbuf[slot].astype(F32)).astype(BF)
            self._send(slot + 4, dg, other, device)

    def _total(self, other):
        direct, folded = (2, 5) if other else (3, 4)
        return (self.part[self.at(0, other)].astype(F32) + self.rbuf[direct].astype(F32)
                + self.rbuf[folded].astype(F32))

    def cross(self):
        self._wait(2)
        self._wait(5)
        self.part[self.at(0, True)] = self._total(True).astype(BF)
        self._send(6, 0, True, self.group.pair)

    def result(self):
        self._wait(3)
        self._wait(4)
        own = self._total(False)
        self._wait(6)
        return own + self.rbuf[6].astype(F32)

    def drain(self):
        for c in self.sent:
            c.wait_send()


def kernel(in_ref, pre_ref, w1_ref, w2_ref, og_ref, dxv, out1, out2,
           og_all, in_all, act_all, pre_all, pre_loc, slope, w1, w2, part, inp, rbuf, rbufx, w1t, w2t,
           g_ss, g_rs, r_ss, r_rs, k_ss, k_rs, l_sem):
    r, c = lax.axis_index("row"), lax.axis_index("col")
    x, zl = r % 4, r // 4
    y, zh, k = c // 4, (c // 2) % 2, c % 2
    mate = (r, c + 1 - 2 * k)
    by_row = Group(x, zl, lambda g, h: (h * 4 + g, c), lambda g, h: h * 4 + g)
    by_col = Group(y, zh, lambda g, h: (r, g * 4 + h * 2 + k), lambda g, h: g * 2 + h)
    mine_row = pl.ds(pl.multiple_of(r * T, T), T)
    mine_col = pl.ds(pl.multiple_of(by_col.block(0, False) * T, T), T)

    def units(core):
        return pl.ds(pl.multiple_of(core * U, U), U)

    loads = [
        pltpu.make_async_copy(pre_ref.at[:, units(k)], pre_loc.at[k], l_sem.at[0]),
        pltpu.make_async_copy(og_ref.at[pl.ds(0, T)], og_all.at[k, 0, mine_row], l_sem.at[1]),
        pltpu.make_async_copy(og_ref.at[pl.ds(T, T)], og_all.at[k, 1, mine_row], l_sem.at[2]),
        pltpu.make_async_copy(w2_ref.at[units(k)], w2.at[k], l_sem.at[3]),
        pltpu.make_async_copy(in_ref.at[pl.ds(0, T)], in_all.at[0, mine_row], l_sem.at[4]),
        pltpu.make_async_copy(in_ref.at[pl.ds(T, T)], in_all.at[1, mine_row], l_sem.at[5]),
        pltpu.make_async_copy(w1_ref, w1, l_sem.at[6]),
    ]
    for load in loads[:4]:
        load.start()

    barrier = pltpu.get_barrier_semaphore()
    friends = (mate, by_row.above, by_row.below, by_row.pair, by_col.above, by_col.below, by_col.pair)
    for friend in friends:
        pl.semaphore_signal(barrier, inc=1, device_id=friend, device_id_type=MESH)
    pl.semaphore_wait(barrier, len(friends))

    halves = (0, 1)
    og = [PairFirst(by_row, og_all.at[k, s], og_all.at[1 - k, s], mate, g_ss.at[s], g_rs.at[s],
                    og_ref.at[pl.ds(s * T, T)]) for s in halves]
    xs = [PairFirst(by_row, in_all.at[s], None, None, g_ss.at[2 + s], g_rs.at[2 + s],
                    in_ref.at[pl.ds(s * T, T)]) for s in halves]
    act = [RingFirst(by_col, act_all.at[k, f], act_all.at[1 - k, f], mate, g_ss.at[4 + f], g_rs.at[4 + f])
           for f in halves]
    pre = [PairFirst(by_col, pre_all.at[k, s], pre_all.at[1 - k, s], mate, g_ss.at[6 + s], g_rs.at[6 + s])
           for s in halves]
    hid = [Scatter(by_col, part.at[s], rbuf.at[s], r_ss.at[s], r_rs.at[s]) for s in halves]
    dx = [Scatter(by_row, inp.at[s], rbufx.at[s], r_ss.at[2 + s], r_rs.at[2 + s]) for s in halves]

    to_mate = [
        pltpu.make_async_remote_copy(
            pre_ref.at[:, units(1 - k)], pre_loc.at[k], k_ss.at[0], k_rs.at[0], mate, MESH),
        pltpu.make_async_remote_copy(w2_ref.at[units(1 - k)], w2.at[k], k_ss.at[1], k_rs.at[1], mate, MESH),
    ]

    def activate(f):
        def some(n, _):
            at = pl.ds(pl.multiple_of(f * W + n * 256, 256), 256)
            to = pl.ds(pl.multiple_of(n * 256, 256), 256)
            for s in halves:
                a = pre_loc[s, :, at].astype(F32)
                t = jnp.tanh(ROOT * (a + CUBE * (a * a * a)))
                act_all[k, f, s, mine_col, to] = (0.5 * a * (1.0 + t)).astype(BF)
                slope[s, :, at] = 0.5 * (1.0 + t) + 0.5 * a * (1.0 - t * t) * (ROOT * (1.0 + 3.0 * CUBE * (a * a)))
            return 0

        lax.fori_loop(0, W // 256, some, 0)

    def pre_grad(s):
        grad = hid[s].result().astype(BF).astype(F32)
        pre_all[k, s, mine_col] = (slope[s] * grad).astype(BF)

    def hidden(s, dg):
        at = pl.ds(pl.multiple_of(((y + dg) % 4) * 2 * T, 2 * T), 2 * T)

        for n in range(U // 256):
            to = pl.ds(n * 256, 256)
            part[s, at, to] = (dot(og_all[0, s, at], w2t[0, :, to]) + dot(og_all[1, s, at], w2t[1, :, to])).astype(BF)

    def input_part(s, dg):
        one, two = dx[s].at(dg, False), dx[s].at(dg, True)

        left = [jnp.concatenate([pre_all[core, s, one], pre_all[core, s, two]], axis=0) for core in (0, 1)]
        for n in range(W // 256):
            to = pl.ds(n * 256, 256)
            total = sum(dot(left[core], w1t[pl.ds(core * U, U), to]) for core in (0, 1)).astype(BF)
            inp[s, one, to] = total[:T]
            inp[s, two, to] = total[T:]

    def second_grad(n):
        at = pl.ds(n * W, W)
        total = sum(tl_dot(act_all[n // 2, n % 2, s], og_all[k, s]) for s in halves)
        out2[at] = total.astype(BF)

    def first_grad(n):
        at = pl.ds(n * W, W)
        total = sum(tl_dot(in_all[s], pre_all[n // 2, s, :, pl.ds((n % 2) * W, W)]) for s in halves)
        out1[:, at] = total.astype(BF)

    def input_grad(s):
        dxv[pl.ds(s * T, T)] = dx[s].result().astype(BF)

    og[0].start()
    to_mate[0].start()
    loads[0].wait()
    to_mate[0].wait_recv()
    activate(0)
    act[0].start()
    activate(1)
    act[1].start()
    to_mate[1].start()
    for load in loads[4:]:
        load.start()
    og[0].take(0, 1, 2)
    act[0].give_own()
    loads[3].wait()
    w2t[k] = w2[k].T
    og[0].take(4, 3)
    og[1].start()
    act[1].give_own()
    to_mate[1].wait_recv()
    w2t[1 - k] = w2[1 - k].T
    og[0].take(5, 6)
    act[0].take_near()
    act[0].give_near()
    loads[1].wait()
    og[0].take_mate()

    hidden(0, 2)
    hid[0].far()
    og[1].take(0, 1, 2)
    hidden(0, 1)
    hidden(0, 3)
    hid[0].near()
    act[1].take_near()
    act[0].take_far()
    og[1].take(4, 3)
    hidden(0, 0)
    og[1].take(5, 6)
    hid[0].fold()
    act[1].give_near()
    xs[0].start()
    act[0].take_pair(0, 1, 2)
    loads[2].wait()
    og[1].take_mate()
    hidden(1, 2)
    hid[1].far()
    hidden(1, 1)
    hidden(1, 3)
    hid[1].near()
    hidden(1, 0)
    act[1].take_far()
    hid[0].cross()
    xs[0].take(0, 1, 2)
    xs[1].start()
    hid[1].fold()
    pre_grad(0)
    pre[0].start()
    xs[0].take(4, 3)
    hid[1].cross()
    pre[0].take(0, 1, 2)
    xs[1].take(0, 1, 2)
    pre_grad(1)
    pre[1].start()
    pre[0].take(4, 3)
    xs[0].take(5, 6)
    xs[1].take(4, 3)
    loads[6].wait()
    w1t[...] = w1[...].T
    act[1].take_pair(0, 1, 2)
    pre[0].take(5, 6)
    pre[1].take(0, 1, 2)
    act[0].give_far()
    act[1].give_far()
    pre[0].take_mate()

    input_part(0, 2)
    dx[0].far()
    input_part(0, 1)
    input_part(0, 3)
    dx[0].near()
    pre[1].take(4, 3)
    input_part(0, 0)
    xs[1].take(5, 6)
    dx[0].fold()
    act[0].take_pair(3)
    act[1].take_pair(3)
    act[0].take_mate()
    second_grad(0)
    act[1].take_mate()
    second_grad(1)
    pre[1].take(5, 6)
    dx[0].cross()
    pre[1].take_mate()
    input_part(1, 2)
    dx[1].far()
    input_part(1, 1)
    input_part(1, 3)
    dx[1].near()
    input_part(1, 0)
    input_grad(0)
    loads[4].wait()
    loads[5].wait()
    first_grad(0)
    dx[1].fold()
    first_grad(1)
    first_grad(2)
    dx[1].cross()
    first_grad(3)
    second_grad(2)
    second_grad(3)
    input_grad(1)
    for item in (*og, *xs, *act, *pre, *hid, *dx):
        item.drain()
    for copy in to_mate:
        copy.wait_send()


def write_out(dx, dw1, dw2, dx_out, dw1_out, dw2_out, sems):
    copies = [
        pltpu.make_async_copy(src, dst, sems.at[i])
        for i, (src, dst) in enumerate(((dw1, dw1_out), (dw2, dw2_out), (dx, dx_out)))
    ]
    for copy in copies:
        copy.start()
    for copy in copies:
        copy.wait()


def local(inputs, pre_act, w_first, w_second, out_grad):
    sem = pltpu.SemaphoreType.DMA
    vm = lambda *shape, dtype=BF: pltpu.VMEM(shape, dtype)
    results = pl.pallas_call(
        kernel,
        out_shape=(
            pltpu.VMEM((2 * T, W), BF),
            pltpu.VMEM((W, 2 * U), BF),
            pltpu.VMEM((2 * U, W), BF),
        ),
        in_specs=[pl.BlockSpec(memory_space=pl.ANY)] * 5,
        out_specs=[pl.BlockSpec(memory_space=pltpu.VMEM)] * 3,
        scratch_shapes=[
            vm(2, 2, HALF, W),
            vm(2, HALF, W),
            vm(2, 2, 2, HALF, W),
            vm(2, 2, HALF, U),
            vm(2, T, U),
            vm(2, T, U, dtype=F32),
            vm(W, 2 * U),
            vm(2, U, W),
            vm(2, HALF, U),
            vm(2, HALF, W),
            vm(2, 7, T, U),
            vm(2, 7, T, W),
            vm(2 * U, W),
            vm(2, W, U),
            sem((8, 16)), sem((8, 16)), sem((4, 7)), sem((4, 7)), sem((2,)), sem((2,)), sem((7,)),
        ],
        compiler_params=pltpu.CompilerParams(
            collective_id=0, has_side_effects=True, vmem_limit_bytes=50 * 2**20
        ),
        cost_estimate=pl.CostEstimate(flops=19_327_352_832, bytes_accessed=20_000_000, transcendentals=400_000),
        name="ffn_back",
    )(inputs, pre_act, w_first, w_second, out_grad)
    return pl.pallas_call(
        write_out,
        out_shape=[jax.ShapeDtypeStruct(array.shape, BF) for array in results],
        in_specs=[pl.BlockSpec(memory_space=pltpu.VMEM)] * 3,
        out_specs=[pl.BlockSpec(memory_space=pl.ANY)] * 3,
        scratch_shapes=[sem((3,))],
        compiler_params=pltpu.CompilerParams(vmem_limit_bytes=1024 * 1024),
        name="write_out",
    )(*results)


def solution(mesh):
    placed = (P("row", "col"), P("col", "row"), P("col", "row"), P("row", "col"), P("row", "col"))
    return jax.shard_map(
        local,
        mesh=mesh,
        in_specs=placed,
        out_specs=(P("row", "col"), P("col", "row"), P("row", "col")),
        check_vma=False,
    )
```

time: 372 us -> 105 us (0.28); the launches traced: 368 us -> 105 us
  waiting for transfers between devices: 306 us -> 0 us
  Pallas kernels: 0 us -> 104 us
  matrix products: 37.5 us -> 0 us
  between operations: 14.1 us -> 0.8 us
  local copies, waits for them, and re-layouts: 6.74 us -> 0 us
    all_gather x4 -> x0, waiting for transfers between devices: 184 us -> none  [the longest x1 63.9 us: local(): grad_piece = lax.all_gather(pre_grad, 'col', axis=0, tiled=True)]
    reduce_scatter x2 -> x0, waiting for transfers between devices: 121 us -> none  [the longest x1 93.9 us: local(): lax.psum_scatter(times_transposed(grad_all, w_second).astype(jnp.bfloat16...]
    pallas_call x0 -> x2, Pallas kernels: none -> 104 us  [the longest x1 100 us: local(): pl.pallas_call(kernel, out_shape=(pltpu.VMEM((2 * T, W), BF), pltpu.VMEM(...]
    dot_general x4 -> x0, matrix products: 37.5 us -> none  [the longest x2 18.8 us: contract_rows(): lax.dot_general(left, right, (((0,), (0,)), ((), ())), preferred_element_...]
    unnamed x5 -> x0, local copies, waits for them, and re-layouts: 6.74 us -> none
  transfers between devices with their start and end apart: 6 -> 0, of which waited for: 6 -> 0; matrix products, arithmetic and copies ran while one was open for 10% -> 0% of each run, Pallas kernels for 0% -> 0%
where the time goes in v2:
time: 105 us
  Pallas kernels  104 us (99%)
    pallas_call x1, Pallas kernels, local(): pl.pallas_call(kernel, out_shape=(pltpu.VMEM((2 * T, W), BF), pltpu.VMEM(...  100 us
    pallas_call x1, Pallas kernels, local(): pl.pallas_call(write_out, out_shape=[jax.ShapeDtypeStruct(array.shape, BF...  3.77 us

profile of v2, /device:TPU:1, one launch (start us, length us, event | category | flops | bytes accessed | tf_op | source)
XLA Modules:
  0.0 104.6 jit_solution(4465506148999129788)
XLA Ops:
  0.6 100.1 %ffn_back.1 = (bf16[128,768]{1,0:T(8,128)(2,1)S(1)}, bf16[768,3072]{1,0:T(8,128)(2,1)S(1)}, bf16[3072,768]{1,0:T(8,128)(2,1)S(1)}) custom-call(bf16[128,768]{1,0:T(8,128)(2,1)} %in_ref.1, bf16[64,3072]{1,0:T(8,128)(2,1)} %pre_ref.1, bf16[768,3072]{1,0:T(8,128)(2,1)} %w1_ref.1, bf16[3072,768]{1,0:T(8,128)(2,1)} %w2_ref.1, bf16[128,768]{1,0:T(8,128)(2,1)} %og_ref.1), custom_call_target="tpu_custom_call" | custom-call | flops 19327352832 | bytes 20000000 | tf_op jit(solution)/shard_map/ffn_back/pallas_call | solution.py:422
  100.7 3.8 %write_out.1 = (bf16[128,768]{1,0:T(8,128)(2,1)}, bf16[768,3072]{1,0:T(8,128)(2,1)}, bf16[3072,768]{1,0:T(8,128)(2,1)}) custom-call(bf16[128,768]{1,0:T(8,128)(2,1)S(1)} %get-tuple-element.6.dx, bf16[768,3072]{1,0:T(8,128)(2,1)S(1)} %get-tuple-element.7.dw1, bf16[3072,768]{1,0:T(8,128)(2,1)S(1)} %get-tuple-element.8.dw2), custom_call_target="tpu_custom_call" | custom-call | tf_op jit(solution)/shard_map/write_out/pallas_call | solution.py:454

commit v3 on v0

v3 whole, which is shorter than its diff:
```python
import jax
import jax.numpy as jnp
from jax import lax
from jax.experimental import pallas as pl
from jax.experimental.pallas import tpu as pltpu
from jax.sharding import PartitionSpec as P

MESH = pl.DeviceIdType.MESH
N = 1024
T = 128
PARTS = ((0, 48), (48, 48), (96, 32))
XPARTS = ((0, 64), (64, 64))
W = 768
U = 1536
F = 2
V = U // F
BF = jnp.bfloat16
F32 = jnp.float32
ROOT = 0.7978845608028654
CUBE = 0.044715


def dot(left, right):
    return jnp.dot(left, right, preferred_element_type=F32)


def tl_dot(left, right):
    return lax.dot_general(left, right, (((0,), (0,)), ((), ())), preferred_element_type=F32)


class Group:
    def __init__(self, g, h, device, block):
        self.g, self.h = g, h
        self.above, self.below, self.pair = device((g + 1) % 4, h), device((g + 3) % 4, h), device(g, 1 - h)
        self.block = lambda dg, other: block((g + dg) % 4, (1 - h) if other else h)


def span(group, owner, part):
    start, size = part
    return pl.ds(pl.multiple_of(group.block(*owner) * T + start, 16), size)


OWN, PAIR = (0, False), (0, True)
BELOW, ABOVE, FAR = (3, False), (1, False), (2, False)
PAIR_BELOW, PAIR_ABOVE, PAIR_FAR = (3, True), (1, True), (2, True)


class Gather:
    def __init__(self, group, part, buf, mate_buf, mate, ssem, rsem, own_src=None):
        self.group, self.part, self.buf, self.mate_buf, self.mate = group, part, buf, mate_buf, mate
        self.ssem, self.rsem, self.own_src = ssem, rsem, own_src
        self.sent = []

    def _ref(self, buf, owner, half=None):
        start, size = self.part
        if half is not None:
            start, size = start + half * (size // 2), size // 2
        return buf.at[span(self.group, owner, (start, size))]

    def _copy(self, slot, owner, device, half=None):
        ref = self._ref(self.buf, owner, half)
        own = owner == OWN and self.own_src is not None
        return pltpu.make_async_remote_copy(
            self.own_src if own else ref, ref, self.ssem.at[slot], self.rsem.at[slot], device, MESH)

    def _send(self, slot, owner, device, half=None):
        c = self._copy(slot, owner, device, half)
        c.start()
        self.sent.append(c)

    def _wait(self, slot, owner, half=None):
        self._copy(slot, owner, self.group.pair, half).wait_recv()

    def _take(self, slot, owner):
        self._wait(slot, owner)
        self._mate(owner)

    def _mate(self, owner):
        if self.mate is not None:
            self._send(8 + owner[0] * 2 + int(owner[1]), owner, self.mate)

    def give_mate(self):
        self._mate(OWN)

    def take_mate(self):
        for dg in range(4):
            for other in (False, True):
                ref, slot = self._ref(self.mate_buf, (dg, other)), 8 + dg * 2 + int(other)
                pltpu.make_async_remote_copy(
                    ref, ref, self.ssem.at[slot], self.rsem.at[slot], self.mate, MESH).wait_recv()

    def drain(self):
        for c in self.sent:
            c.wait_send()

    def send_own_up(self):
        self._send(0, OWN, self.group.above)

    def send_own_down(self):
        self._send(1, OWN, self.group.below)

    def send_own_pair(self):
        self._send(2, OWN, self.group.pair)

    def take_up(self):
        self._take(0, BELOW)

    def take_down(self):
        self._take(1, ABOVE)

    def take_pair(self):
        self._take(2, PAIR)

    def send_half_up(self):
        self._send(3, BELOW, self.group.above, 0)

    def send_half_down(self):
        self._send(4, ABOVE, self.group.below, 1)

    def take_far(self):
        self._wait(3, FAR, 0)
        self._wait(4, FAR, 1)
        self._mate(FAR)

    def send_pair_up(self):
        self._send(5, BELOW, self.group.pair)

    def send_pair_down(self):
        self._send(6, ABOVE, self.group.pair)

    def send_pair_far(self):
        self._send(7, FAR, self.group.pair)

    def take_pair_up(self):
        self._take(5, PAIR_BELOW)

    def take_pair_down(self):
        self._take(6, PAIR_ABOVE)

    def take_pair_far(self):
        self._take(7, PAIR_FAR)

    def send_other_up(self):
        self._send(5, PAIR, self.group.above)

    def send_other_down(self):
        self._send(6, PAIR, self.group.below)

    def take_other_up(self):
        self._take(5, PAIR_BELOW)

    def take_other_down(self):
        self._take(6, PAIR_ABOVE)

    def send_far_up(self):
        self._send(3, BELOW, self.group.above)

    def send_far_down(self):
        self._send(4, PAIR_ABOVE, self.group.below)

    def take_far_up(self):
        self._take(3, FAR)

    def take_far_down(self):
        self._take(4, PAIR_FAR)

    def start(self):
        self.send_own_pair()
        self.send_own_up()
        self.send_own_down()
        self.give_mate()

    def take(self, step):
        if step == 0:
            self._wait(2, PAIR)
            self.send_other_up()
            self.send_other_down()
            self._mate(PAIR)
        elif step == 1:
            self._wait(0, BELOW)
            self.send_far_up()
            self._mate(BELOW)
        elif step == 2:
            self.take_down()
        elif step == 3:
            self.take_other_up()
        elif step == 4:
            self._wait(6, PAIR_ABOVE)
            self.send_far_down()
            self._mate(PAIR_ABOVE)
        elif step == 5:
            self.take_far_up()
        else:
            self.take_far_down()


class Scatter:
    def __init__(self, group, part, terms, rbuf, ssem, rsem):
        self.group, self.part, self.terms, self.ssem, self.rsem = group, part, terms, ssem, rsem
        self.rbuf = rbuf.at[:, pl.ds(*part)]
        self.sent = []

    def at(self, dg, other):
        return span(self.group, (dg, other), self.part)

    def _copy(self, slot, at, device):
        return pltpu.make_async_remote_copy(
            self.terms.at[at], self.rbuf.at[slot], self.ssem.at[slot], self.rsem.at[slot], device, MESH)

    def _send(self, slot, dg, other, device):
        c = self._copy(slot, self.at(dg, other), device)
        c.start()
        self.sent.append(c)

    def _wait(self, slot):
        self._copy(slot, self.at(0, False), self.group.pair).wait_recv()

    def far(self):
        self._send(0, 2, False, self.group.above)
        self._send(1, 2, True, self.group.below)

    def near(self):
        self._send(2, 1, True, self.group.above)
        self._send(3, 3, False, self.group.below)

    def fold(self, way):
        dg, other, device = ((1, False, self.group.above), (3, True, self.group.below))[way]
        self._wait(way)
        at = self.at(dg, other)
        self.terms[at] = (self.terms[at].astype(F32) + self.rbuf[way].astype(F32)).astype(BF)
        self._send(way + 4, dg, other, device)

    def _total(self, other):
        direct, folded = (2, 5) if other else (3, 4)
        return (self.terms[self.at(0, other)].astype(F32) + self.rbuf[direct].astype(F32)
                + self.rbuf[folded].astype(F32))

    def cross(self):
        self._wait(2)
        self._wait(5)
        self.terms[self.at(0, True)] = self._total(True).astype(BF)
        self._send(6, 0, True, self.group.pair)

    def result(self):
        self._wait(3)
        self._wait(4)
        own = self._total(False)
        self._wait(6)
        return own + self.rbuf[6].astype(F32)

    def drain(self):
        for c in self.sent:
            c.wait_send()


def kernel(in_ref, pre_ref, w1_ref, w2_ref, og_ref, dxv, out1, out2,
           og_all, in_all, act_all, pre_all, pre_loc, slope, w1, w2, terms, inp, rbuf, rbufx, w1t, w2t,
           og_ss, og_rs, xs_ss, xs_rs, act_ss, act_rs, pre_ss, pre_rs, hid_ss, hid_rs, dx_ss, dx_rs, k_ss, k_rs, l_sem):
    r, c = lax.axis_index("row"), lax.axis_index("col")
    x, zl = r % 4, r // 4
    y, zh, k = c // 4, (c // 2) % 2, c % 2
    mate = (r, c + 1 - 2 * k)
    by_row = Group(x, zl, lambda g, h: (h * 4 + g, c), lambda g, h: h * 4 + g)
    by_col = Group(y, zh, lambda g, h: (r, g * 4 + h * 2 + k), lambda g, h: g * 2 + h)
    mine_row = span(by_row, OWN, (0, T))
    mine_col = span(by_col, OWN, (0, T))
    own64 = pl.ds(pl.multiple_of(k * (T // 2), T // 2), T // 2)

    def units(core):
        return pl.ds(pl.multiple_of(core * U, U), U)

    loads = [
        pltpu.make_async_copy(pre_ref.at[:, units(k)], pre_loc.at[own64], l_sem.at[0]),
        pltpu.make_async_copy(og_ref, og_all.at[k, mine_row], l_sem.at[1]),
        pltpu.make_async_copy(w2_ref.at[units(k)], w2.at[k], l_sem.at[2]),
        pltpu.make_async_copy(in_ref, in_all.at[mine_row], l_sem.at[3]),
        pltpu.make_async_copy(w1_ref, w1, l_sem.at[4]),
    ]
    for load in loads[:3]:
        load.start()

    barrier = pltpu.get_barrier_semaphore()
    friends = (mate, by_row.above, by_row.below, by_row.pair, by_col.above, by_col.below, by_col.pair)
    for friend in friends:
        pl.semaphore_signal(barrier, inc=1, device_id=friend, device_id_type=MESH)
    pl.semaphore_wait(barrier, len(friends))

    og = [Gather(by_row, part, og_all.at[k], og_all.at[1 - k], mate, og_ss.at[i], og_rs.at[i], og_ref.at[pl.ds(*part)])
          for i, part in enumerate(PARTS)]
    xs = [Gather(by_row, part, in_all, None, None, xs_ss.at[i], xs_rs.at[i], in_ref.at[pl.ds(*part)])
          for i, part in enumerate(XPARTS)]
    act = [Gather(by_col, (0, T), act_all.at[k, f], act_all.at[1 - k, f], mate, act_ss.at[f], act_rs.at[f])
           for f in range(F)]
    pre = [Gather(by_col, part, pre_all.at[k], pre_all.at[1 - k], mate, pre_ss.at[i], pre_rs.at[i])
           for i, part in enumerate(PARTS)]
    hid = [Scatter(by_col, part, terms, rbuf, hid_ss.at[i], hid_rs.at[i]) for i, part in enumerate(PARTS)]
    dx = [Scatter(by_row, part, inp, rbufx, dx_ss.at[i], dx_rs.at[i]) for i, part in enumerate(PARTS)]

    to_mate = [
        pltpu.make_async_remote_copy(
            pre_ref.at[:, units(1 - k)], pre_loc.at[own64], k_ss.at[0], k_rs.at[0], mate, MESH),
        pltpu.make_async_remote_copy(w2_ref.at[units(1 - k)], w2.at[k], k_ss.at[1], k_rs.at[1], mate, MESH),
    ]

    def activate(f):
        def some(n, _):
            at = pl.ds(pl.multiple_of(f * V + n * 128, 128), 128)
            to = pl.ds(pl.multiple_of(n * 128, 128), 128)
            a = pre_loc[:, at].astype(F32)
            t = jnp.tanh(ROOT * (a + CUBE * (a * a * a)))
            act_all[k, f, mine_col, to] = (0.5 * a * (1.0 + t)).astype(BF)
            slope[:, at] = 0.5 * (1.0 + t) + 0.5 * a * (1.0 - t * t) * (ROOT * (1.0 + 3.0 * CUBE * (a * a)))
            return 0

        lax.fori_loop(0, V // 128, some, 0)

    def pre_grad(s):
        grad = hid[s].result().astype(BF).astype(F32)
        pre_all[k, span(by_col, OWN, PARTS[s])] = (slope[pl.ds(*PARTS[s])] * grad).astype(BF)

    def blocks(scatter, dgs):
        return [scatter.at(dg, other) for dg in dgs for other in (False, True)]

    def product(scatter, dgs, lefts, rights, width, out):
        places, size = blocks(scatter, dgs), scatter.part[1]
        lefts = [jnp.concatenate([left[at] for at in places], axis=0) for left in lefts]
        for n in range(width // 256):
            to = pl.ds(n * 256, 256)
            total = sum(dot(left, right[:, to]) for left, right in zip(lefts, rights)).astype(BF)
            for i, at in enumerate(places):
                out[at, to] = total[i * size:(i + 1) * size]

    def hidden(s, *dgs):
        product(hid[s], dgs, [og_all.at[core] for core in (0, 1)], [w2t.at[core] for core in (0, 1)], U, terms)

    def input_part(s, *dgs):
        product(dx[s], dgs, [pre_all.at[core] for core in (0, 1)], [w1t.at[pl.ds(core * U, U)] for core in (0, 1)], W, inp)

    def second_grad(core, f):
        out2[pl.ds(core * U + f * V, V)] = tl_dot(act_all[core, f], og_all[k]).astype(BF)

    def first_grad(n):
        out1[:, pl.ds(n * W, W)] = tl_dot(in_all[...], pre_all[n // 2, :, pl.ds((n % 2) * W, W)]).astype(BF)

    def input_grad(s):
        dxv[pl.ds(*PARTS[s])] = dx[s].result().astype(BF)

    og[0].start()
    to_mate[0].start()
    loads[0].wait()
    to_mate[0].wait_recv()
    activate(0)
    act[0].send_own_down()
    act[0].send_own_up()
    for load in loads[3:]:
        load.start()
    act[0].send_own_pair()
    og[0].take(0)
    og[0].take(1)
    to_mate[1].start()
    activate(1)
    og[0].take(2)
    act[1].send_own_down()
    act[1].send_own_up()
    xs[0].send_own_up()
    og[0].take(4)
    og[1].start()
    og[0].take(5)
    xs[1].send_own_pair()
    act[0].take_pair()
    act[1].send_own_pair()
    act[0].take_up()
    act[0].take_down()
    act[0].send_half_down()
    og[0].take(3)
    og[0].take(6)
    loads[2].wait()
    w2t[k] = w2[k].T
    og[1].take(0)
    act[0].send_half_up()
    xs[0].take_up()
    to_mate[1].wait_recv()
    w2t[1 - k] = w2[1 - k].T
    act[1].take_down()
    act[1].send_half_down()
    act[1].take_up()
    act[1].send_half_up()
    xs[1].take_pair()
    og[0].take_mate()
    loads[1].wait()
    hidden(0, 2)
    hid[0].far()
    xs[0].send_own_pair()
    og[1].take(3)
    act[0].give_mate()
    og[1].take(1)
    og[1].take(4)
    og[2].start()
    hidden(0, 1, 3, 0)
    hid[0].near()
    act[1].send_pair_up()
    hid[0].fold(1)
    og[1].take(2)
    og[2].take(1)
    og[1].take(6)
    og[1].take(5)
    xs[0].take_pair()
    act[1].send_pair_down()
    hid[0].fold(0)
    og[2].take(0)
    og[1].take_mate()
    hidden(1, 2)
    hid[1].far()
    xs[0].send_far_up()
    xs[1].send_other_down()
    hidden(1, 1, 3, 0)
    hid[1].near()
    og[2].take(5)
    og[2].take(2)
    hid[0].cross()
    og[2].take(3)
    xs[0].send_other_up()
    og[2].take(4)
    xs[1].take_other_down()
    xs[1].send_other_up()
    xs[1].send_far_down()
    hid[1].fold(1)
    act[1].take_far()
    xs[0].send_other_down()
    act[0].send_pair_down()
    og[2].take(6)
    act[1].take_pair_down()
    xs[0].send_own_down()
    hid[1].fold(0)
    og[2].take_mate()
    hidden(2, 2)
    hid[2].far()
    hidden(2, 1, 3, 0)
    hid[2].near()
    pre_grad(0)
    pre[0].start()
    hid[1].cross()
    hid[2].fold(0)
    act[1].send_pair_far()
    pre[0].take(0)
    act[0].take_far()
    pre[0].take(2)
    act[1].take_pair()
    hid[2].fold(1)
    act[1].take_pair_up()
    xs[1].send_own_up()
    xs[1].take_far_down()
    xs[0].take_other_down()
    pre_grad(1)
    pre[1].start()
    xs[1].send_own_down()
    act[1].take_pair_far()
    act[0].take_pair_down()
    loads[4].wait()
    w1t[...] = w1[...].T
    act[1].give_mate()
    hid[2].cross()
    pre[0].take(1)
    xs[0].take_other_up()
    pre[0].take(4)
    pre[1].take(0)
    pre[1].take(1)
    pre_grad(2)
    pre[2].start()
    pre[0].take(3)
    act[1].take_mate()
    xs[0].send_far_down()
    act[0].send_pair_up()
    act[0].send_pair_far()
    second_grad(0, 1)
    pre[0].take(6)
    pre[0].take(5)
    second_grad(1, 1)
    xs[1].take_other_up()
    pre[1].take(4)
    pre[1].take(2)
    pre[2].take(0)
    pre[1].take(3)
    pre[0].take_mate()
    input_part(0, 2)
    dx[0].far()
    input_part(0, 1, 3, 0)
    dx[0].near()
    pre[2].take(2)
    xs[0].take_far_down()
    xs[0].take_down()
    pre[1].take(5)
    pre[1].take(6)
    dx[0].fold(0)
    act[0].take_pair_up()
    dx[0].fold(1)
    xs[1].take_up()
    xs[0].take_far_up()
    xs[1].take_down()
    pre[2].take(1)
    xs[1].send_far_up()
    pre[1].take_mate()
    pre[2].take(4)
    input_part(1, 2)
    dx[1].far()
    act[0].take_pair_far()
    input_part(1, 1, 3, 0)
    dx[1].near()
    act[0].take_mate()
    pre[2].take(3)
    pre[2].take(5)
    dx[0].cross()
    pre[2].take(6)
    dx[1].fold(1)
    second_grad(0, 0)
    pre[2].take_mate()
    loads[3].wait()
    input_part(2, 2)
    dx[2].far()
    input_part(2, 1, 3, 0)
    dx[2].near()
    xs[1].take_far_up()
    first_grad(0)
    dx[1].fold(0)
    dx[2].fold(1)
    dx[1].cross()
    second_grad(1, 0)
    first_grad(1)
    dx[2].fold(0)
    dx[2].cross()
    input_grad(0)
    first_grad(3)
    first_grad(2)
    input_grad(1)
    input_grad(2)
    for item in (*og, *xs, *act, *pre, *hid, *dx):
        item.drain()
    for copy in to_mate:
        copy.wait_send()


def write_out(dx, dw1, dw2, dx_out, dw1_out, dw2_out, sems):
    copies = [
        pltpu.make_async_copy(src, dst, sems.at[i])
        for i, (src, dst) in enumerate(((dw1, dw1_out), (dw2, dw2_out), (dx, dx_out)))
    ]
    for copy in copies:
        copy.start()
    for copy in copies:
        copy.wait()


def local(inputs, pre_act, w_first, w_second, out_grad):
    sem, S, X = pltpu.SemaphoreType.DMA, len(PARTS), len(XPARTS)
    vm = lambda *shape, dtype=BF: pltpu.VMEM(shape, dtype)
    results = pl.pallas_call(
        kernel,
        out_shape=(
            pltpu.VMEM((T, W), BF),
            pltpu.VMEM((W, 2 * U), BF),
            pltpu.VMEM((2 * U, W), BF),
        ),
        in_specs=[pl.BlockSpec(memory_space=pl.ANY)] * 5,
        out_specs=[pl.BlockSpec(memory_space=pltpu.VMEM)] * 3,
        scratch_shapes=[
            vm(2, N, W),
            vm(N, W),
            vm(2, F, N, V),
            vm(2, N, U),
            vm(T, U),
            vm(T, U, dtype=F32),
            vm(W, 2 * U),
            vm(2, U, W),
            vm(N, U),
            vm(N, W),
            vm(7, T, U),
            vm(7, T, W),
            vm(2 * U, W),
            vm(2, W, U),
            sem((S, 16)), sem((S, 16)), sem((X, 7)), sem((X, 7)), sem((F, 16)), sem((F, 16)), sem((S, 16)), sem((S, 16)),
            sem((S, 7)), sem((S, 7)), sem((S, 7)), sem((S, 7)), sem((2,)), sem((2,)), sem((5,)),
        ],
        compiler_params=pltpu.CompilerParams(
            collective_id=0, has_side_effects=True, vmem_limit_bytes=50 * 2**20
        ),
        cost_estimate=pl.CostEstimate(flops=19_327_352_832, bytes_accessed=20_000_000, transcendentals=400_000),
        name="ffn_back",
    )(inputs, pre_act, w_first, w_second, out_grad)
    return pl.pallas_call(
        write_out,
        out_shape=[jax.ShapeDtypeStruct(array.shape, BF) for array in results],
        in_specs=[pl.BlockSpec(memory_space=pltpu.VMEM)] * 3,
        out_specs=[pl.BlockSpec(memory_space=pl.ANY)] * 3,
        scratch_shapes=[sem((3,))],
        compiler_params=pltpu.CompilerParams(vmem_limit_bytes=1024 * 1024),
        name="write_out",
    )(*results)


def solution(mesh):
    placed = (P("row", "col"), P("col", "row"), P("col", "row"), P("row", "col"), P("row", "col"))
    return jax.shard_map(
        local,
        mesh=mesh,
        in_specs=placed,
        out_specs=(P("row", "col"), P("col", "row"), P("row", "col")),
        check_vma=False,
    )
```

time: 372 us -> 98.3 us (0.26)
  waiting for transfers between devices: 306 us -> 0 us
  Pallas kernels: 0 us -> 96.2 us
  matrix products: 37.5 us -> 0 us
  between operations: 14.1 us -> 0.8 us
  local copies, waits for them, and re-layouts: 6.74 us -> 0 us
    all_gather x4 -> x0, waiting for transfers between devices: 184 us -> none  [the longest x1 63.9 us: local(): grad_piece = lax.all_gather(pre_grad, 'col', axis=0, tiled=True)]
    reduce_scatter x2 -> x0, waiting for transfers between devices: 121 us -> none  [the longest x1 93.9 us: local(): lax.psum_scatter(times_transposed(grad_all, w_second).astype(jnp.bfloat16...]
    pallas_call x0 -> x2, Pallas kernels: none -> 96.2 us  [the longest x1 92.4 us: local(): pl.pallas_call(kernel, out_shape=(pltpu.VMEM((T, W), BF), pltpu.VMEM((W,...]
    dot_general x4 -> x0, matrix products: 37.5 us -> none  [the longest x2 18.8 us: contract_rows(): lax.dot_general(left, right, (((0,), (0,)), ((), ())), preferred_element_...]
    unnamed x5 -> x0, local copies, waits for them, and re-layouts: 6.74 us -> none
  transfers between devices with their start and end apart: 6 -> 0, of which waited for: 6 -> 0; matrix products, arithmetic and copies ran while one was open for 10% -> 0% of each run, Pallas kernels for 0% -> 0%
where the time goes in v3:
time: 98.3 us; the launch traced here: 97 us
  Pallas kernels  96.2 us (98%)
    pallas_call x1, Pallas kernels, local(): pl.pallas_call(kernel, out_shape=(pltpu.VMEM((T, W), BF), pltpu.VMEM((W,...  92.4 us
    pallas_call x1, Pallas kernels, local(): pl.pallas_call(write_out, out_shape=[jax.ShapeDtypeStruct(array.shape, BF...  3.77 us

profile of v3, /device:TPU:1, one launch (start us, length us, event | category | flops | bytes accessed | tf_op | source)
XLA Modules:
  0.0 97.0 jit_solution(3013275198503713112)
XLA Ops:
  0.6 92.4 %ffn_back.1 = (bf16[128,768]{1,0:T(8,128)(2,1)S(1)}, bf16[768,3072]{1,0:T(8,128)(2,1)S(1)}, bf16[3072,768]{1,0:T(8,128)(2,1)S(1)}) custom-call(bf16[128,768]{1,0:T(8,128)(2,1)} %in_ref.1, bf16[64,3072]{1,0:T(8,128)(2,1)} %pre_ref.1, bf16[768,3072]{1,0:T(8,128)(2,1)} %w1_ref.1, bf16[3072,768]{1,0:T(8,128)(2,1)} %w2_ref.1, bf16[128,768]{1,0:T(8,128)(2,1)} %og_ref.1), custom_call_target="tpu_custom_call" | custom-call | flops 19327352832 | bytes 20000000 | tf_op jit(solution)/shard_map/ffn_back/pallas_call | solution.py:556
  93.1 3.8 %write_out.1 = (bf16[128,768]{1,0:T(8,128)(2,1)}, bf16[768,3072]{1,0:T(8,128)(2,1)}, bf16[3072,768]{1,0:T(8,128)(2,1)}) custom-call(bf16[128,768]{1,0:T(8,128)(2,1)S(1)} %get-tuple-element.6.dx, bf16[768,3072]{1,0:T(8,128)(2,1)S(1)} %get-tuple-element.7.dw1, bf16[3072,768]{1,0:T(8,128)(2,1)S(1)} %get-tuple-element.8.dw2), custom_call_target="tpu_custom_call" | custom-call | tf_op jit(solution)/shard_map/write_out/pallas_call | solution.py:589

commit v4 on v3

--- a/solution.py
+++ b/solution.py
@@ -12,7 +12,7 @@
 XPARTS = ((0, 64), (64, 64))
 W = 768
 U = 1536
-F = 2
+F = 4
 V = U // F
 BF = jnp.bfloat16
 F32 = jnp.float32
@@ -33,6 +33,7 @@
         self.g, self.h = g, h
         self.above, self.below, self.pair = device((g + 1) % 4, h), device((g + 3) % 4, h), device(g, 1 - h)
         self.block = lambda dg, other: block((g + dg) % 4, (1 - h) if other else h)
+        self.device = lambda dg, other: device((g + dg) % 4, (1 - h) if other else h)
 
 
 def span(group, owner, part):
@@ -43,12 +44,17 @@
 OWN, PAIR = (0, False), (0, True)
 BELOW, ABOVE, FAR = (3, False), (1, False), (2, False)
 PAIR_BELOW, PAIR_ABOVE, PAIR_FAR = (3, True), (1, True), (2, True)
+OTHERS = (FAR, PAIR_FAR, PAIR, BELOW, ABOVE, PAIR_BELOW, PAIR_ABOVE)
+
+
+def seen_from(place):
+    return (4 - place[0]) % 4, place[1]
 
 
 class Gather:
-    def __init__(self, group, part, buf, mate_buf, mate, ssem, rsem, own_src=None):
+    def __init__(self, group, part, buf, mate_buf, mate, ssem, rsem, own_src=None, core=0):
         self.group, self.part, self.buf, self.mate_buf, self.mate = group, part, buf, mate_buf, mate
-        self.ssem, self.rsem, self.own_src = ssem, rsem, own_src
+        self.ssem, self.rsem, self.own_src, self.core = ssem, rsem, own_src, core
         self.sent = []
 
     def _ref(self, buf, owner, half=None):
@@ -163,6 +169,50 @@
 
     def take_far_down(self):
         self._take(4, PAIR_FAR)
+
+    def start_direct(self):
+        for place in OTHERS:
+            self._send(OTHERS.index(seen_from(place)), OWN, self.group.device(*place))
+        self.give_mate()
+
+    def take_direct(self, step):
+        owner = (PAIR, BELOW, ABOVE, PAIR_BELOW, PAIR_ABOVE, FAR, PAIR_FAR)[step]
+        self._take(OTHERS.index(owner), owner)
+
+    def _send_rows(self, slot, device, core):
+        at = self._rows(OWN, core)
+        c = pltpu.make_async_remote_copy(
+            self.buf.at[at], self.buf.at[at], self.ssem.at[slot], self.rsem.at[slot], device, MESH)
+        c.start()
+        self.sent.append(c)
+
+    def _rows(self, owner, core):
+        return pl.ds(pl.multiple_of(self.group.block(*owner) * T + core * (T // 2), T // 2), T // 2)
+
+    def _take_rows(self, slots, owner):
+        for slot, core in zip(slots, (self.core, 1 - self.core)):
+            ref = self.buf.at[self._rows(owner, core)]
+            pltpu.make_async_remote_copy(
+                ref, ref, self.ssem.at[slot], self.rsem.at[slot], self.group.pair, MESH).wait_recv()
+        self._mate(owner)
+
+    def send_mine_up(self):
+        self._send_rows(0, self.group.above, self.core)
+
+    def send_mine_down(self):
+        self._send_rows(1, self.group.below, self.core)
+
+    def send_mates_up(self):
+        self._send_rows(16, self.group.above, 1 - self.core)
+
+    def send_mates_down(self):
+        self._send_rows(17, self.group.below, 1 - self.core)
+
+    def take_up2(self):
+        self._take_rows((0, 16), BELOW)
+
+    def take_down2(self):
+        self._take_rows((1, 17), ABOVE)
 
     def start(self):
         self.send_own_pair()
@@ -215,6 +265,16 @@
     def _wait(self, slot):
         self._copy(slot, self.at(0, False), self.group.pair).wait_recv()
 
+    def direct(self, *dgs):
+        for place in OTHERS + (OWN,):
+            if place[0] in dgs and place != OWN:
+                self._send(OTHERS.index(seen_from(place)), *place, self.group.device(*place))
+
+    def result_direct(self):
+        for slot in range(7):
+            self._wait(slot)
+        return self.terms[self.at(*OWN)].astype(F32) + sum(self.rbuf[slot].astype(F32) for slot in range(7))
+
     def far(self):
         self._send(0, 2, False, self.group.above)
         self._send(1, 2, True, self.group.below)
@@ -280,16 +340,15 @@
         load.start()
 
     barrier = pltpu.get_barrier_semaphore()
-    friends = (mate, by_row.above, by_row.below, by_row.pair, by_col.above, by_col.below, by_col.pair)
+    friends = (mate, by_col.above, by_col.below, by_col.pair) + tuple(by_row.device(*place) for place in OTHERS)
     for friend in friends:
         pl.semaphore_signal(barrier, inc=1, device_id=friend, device_id_type=MESH)
-    pl.semaphore_wait(barrier, len(friends))
-
     og = [Gather(by_row, part, og_all.at[k], og_all.at[1 - k], mate, og_ss.at[i], og_rs.at[i], og_ref.at[pl.ds(*part)])
           for i, part in enumerate(PARTS)]
     xs = [Gather(by_row, part, in_all, None, None, xs_ss.at[i], xs_rs.at[i], in_ref.at[pl.ds(*part)])
           for i, part in enumerate(XPARTS)]
-    act = [Gather(by_col, (0, T), act_all.at[k, f], act_all.at[1 - k, f], mate, act_ss.at[f], act_rs.at[f])
+    act = [Gather(by_col, (0, T), act_all.at[k, f], act_all.at[1 - k, f], mate, act_ss.at[f], act_rs.at[f],
+                  core=k)
            for f in range(F)]
     pre = [Gather(by_col, part, pre_all.at[k], pre_all.at[1 - k], mate, pre_ss.at[i], pre_rs.at[i])
            for i, part in enumerate(PARTS)]
@@ -302,14 +361,17 @@
         pltpu.make_async_remote_copy(w2_ref.at[units(1 - k)], w2.at[k], k_ss.at[1], k_rs.at[1], mate, MESH),
     ]
 
-    def activate(f):
+    def activate(f, core):
+        tokens = pl.ds(pl.multiple_of(core * (T // 2), T // 2), T // 2)
+        own = act[f]._rows(OWN, core)
+
         def some(n, _):
             at = pl.ds(pl.multiple_of(f * V + n * 128, 128), 128)
             to = pl.ds(pl.multiple_of(n * 128, 128), 128)
-            a = pre_loc[:, at].astype(F32)
+            a = pre_loc[tokens, at].astype(F32)
             t = jnp.tanh(ROOT * (a + CUBE * (a * a * a)))
-            act_all[k, f, mine_col, to] = (0.5 * a * (1.0 + t)).astype(BF)
-            slope[:, at] = 0.5 * (1.0 + t) + 0.5 * a * (1.0 - t * t) * (ROOT * (1.0 + 3.0 * CUBE * (a * a)))
+            act_all[k, f, own, to] = (0.5 * a * (1.0 + t)).astype(BF)
+            slope[tokens, at] = 0.5 * (1.0 + t) + 0.5 * a * (1.0 - t * t) * (ROOT * (1.0 + 3.0 * CUBE * (a * a)))
             return 0
 
         lax.fori_loop(0, V // 128, some, 0)
@@ -342,197 +404,246 @@
     def first_grad(n):
         out1[:, pl.ds(n * W, W)] = tl_dot(in_all[...], pre_all[n // 2, :, pl.ds((n % 2) * W, W)]).astype(BF)
 
-    def input_grad(s):
-        dxv[pl.ds(*PARTS[s])] = dx[s].result().astype(BF)
-
-    og[0].start()
+    def input_grad(s, direct=False):
+        dxv[pl.ds(*PARTS[s])] = (dx[s].result_direct() if direct else dx[s].result()).astype(BF)
+
+    loads[0].wait()
+    for f in range(F):
+        activate(f, k)
+    pl.semaphore_wait(barrier, len(friends))
+
     to_mate[0].start()
-    loads[0].wait()
+    act[3].send_mine_down()
+    og[0].start_direct()
+    act[0].send_mine_up()
+    act[1].send_mine_down()
     to_mate[0].wait_recv()
-    activate(0)
-    act[0].send_own_down()
-    act[0].send_own_up()
+    activate(0, 1 - k)
+    to_mate[1].start()
+    act[0].send_mates_up()
+    activate(1, 1 - k)
+    act[2].send_mine_down()
+    act[1].send_mates_down()
+    activate(2, 1 - k)
+    act[2].send_mates_up()
     for load in loads[3:]:
         load.start()
-    act[0].send_own_pair()
-    og[0].take(0)
-    og[0].take(1)
-    to_mate[1].start()
-    activate(1)
-    og[0].take(2)
-    act[1].send_own_down()
-    act[1].send_own_up()
-    xs[0].send_own_up()
-    og[0].take(4)
+    activate(3, 1 - k)
+    act[0].send_mine_down()
     og[1].start()
-    og[0].take(5)
-    xs[1].send_own_pair()
-    act[0].take_pair()
-    act[1].send_own_pair()
-    act[0].take_up()
-    act[0].take_down()
-    act[0].send_half_down()
-    og[0].take(3)
-    og[0].take(6)
+    act[1].send_mine_up()
     loads[2].wait()
     w2t[k] = w2[k].T
-    og[1].take(0)
-    act[0].send_half_up()
-    xs[0].take_up()
+    og[0].take_direct(0)
+    act[3].send_mates_down()
+    act[0].send_mates_down()
+    act[1].send_mates_up()
+    act[0].send_own_pair()
+    act[0].take_up2()
+    act[3].send_mates_up()
+    act[2].send_mates_down()
+    act[1].take_down2()
+    og[0].take_direct(6)
+    xs[0].send_own_pair()
+    xs[1].send_own_pair()
+    og[0].take_direct(5)
+    act[3].send_mine_up()
     to_mate[1].wait_recv()
     w2t[1 - k] = w2[1 - k].T
-    act[1].take_down()
+    og[0].take_direct(2)
+    act[0].send_half_up()
+    xs[1].send_own_up()
     act[1].send_half_down()
-    act[1].take_up()
+    og[0].take_direct(1)
+    act[1].take_up2()
+    act[2].send_mine_up()
+    act[3].take_down2()
     act[1].send_half_up()
-    xs[1].take_pair()
+    og[0].take_direct(3)
+    og[0].take_direct(4)
+    act[0].take_down2()
+    act[1].send_own_pair()
+    act[3].send_half_down()
+    act[0].send_half_down()
+    og[1].take(0)
     og[0].take_mate()
     loads[1].wait()
     hidden(0, 2)
     hid[0].far()
-    xs[0].send_own_pair()
-    og[1].take(3)
-    act[0].give_mate()
-    og[1].take(1)
-    og[1].take(4)
-    og[2].start()
     hidden(0, 1, 3, 0)
     hid[0].near()
+    og[1].take(4)
+    og[1].take(1)
+    og[1].take(3)
+    og[2].start()
+    act[0].send_pair_up()
+    hid[0].fold(1)
+    act[0].send_pair_down()
+    xs[1].take_up()
+    hid[0].fold(0)
+    og[1].take(6)
     act[1].send_pair_up()
-    hid[0].fold(1)
-    og[1].take(2)
-    og[2].take(1)
-    og[1].take(6)
     og[1].take(5)
     xs[0].take_pair()
-    act[1].send_pair_down()
-    hid[0].fold(0)
+    og[1].take(2)
+    xs[1].take_pair()
+    act[0].take_far()
+    og[2].take(1)
     og[2].take(0)
     og[1].take_mate()
     hidden(1, 2)
     hid[1].far()
-    xs[0].send_far_up()
-    xs[1].send_other_down()
+    loads[4].wait()
+    w1t[...] = w1[...].T
+    act[3].take_up2()
     hidden(1, 1, 3, 0)
     hid[1].near()
+    hid[0].cross()
+    xs[1].send_other_down()
+    og[2].take(4)
+    og[2].take(3)
+    act[3].send_pair_down()
+    act[0].send_pair_far()
     og[2].take(5)
+    act[3].send_half_up()
+    xs[0].send_other_down()
+    hid[1].fold(1)
+    hid[1].fold(0)
+    og[2].take(6)
+    act[1].give_mate()
+    pre_grad(0)
+    pre[0].start()
     og[2].take(2)
-    hid[0].cross()
-    og[2].take(3)
-    xs[0].send_other_up()
-    og[2].take(4)
-    xs[1].take_other_down()
-    xs[1].send_other_up()
-    xs[1].send_far_down()
-    hid[1].fold(1)
-    act[1].take_far()
-    xs[0].send_other_down()
-    act[0].send_pair_down()
-    og[2].take(6)
-    act[1].take_pair_down()
-    xs[0].send_own_down()
-    hid[1].fold(0)
     og[2].take_mate()
+    act[0].give_mate()
     hidden(2, 2)
     hid[2].far()
+    hid[1].cross()
     hidden(2, 1, 3, 0)
     hid[2].near()
-    pre_grad(0)
-    pre[0].start()
-    hid[1].cross()
+    act[0].take_pair_up()
+    act[3].give_mate()
+    act[1].take_pair_up()
+    act[1].send_pair_down()
+    pre[0].take(0)
+    xs[1].send_far_up()
+    act[1].take_pair()
+    loads[3].wait()
+    xs[0].send_own_up()
+    act[1].take_far()
+    hid[2].fold(1)
+    xs[1].send_own_down()
+    act[0].take_pair_down()
+    act[2].take_down2()
+    act[2].take_up2()
+    act[0].take_pair()
+    act[3].send_own_pair()
+    act[3].send_pair_up()
+    act[3].take_far()
+    pre[0].take(2)
+    pre[0].take(1)
+    xs[0].send_other_up()
     hid[2].fold(0)
-    act[1].send_pair_far()
-    pre[0].take(0)
-    act[0].take_far()
-    pre[0].take(2)
-    act[1].take_pair()
-    hid[2].fold(1)
-    act[1].take_pair_up()
-    xs[1].send_own_up()
-    xs[1].take_far_down()
-    xs[0].take_other_down()
+    act[0].take_pair_far()
+    pre[0].take(4)
+    act[0].take_mate()
     pre_grad(1)
     pre[1].start()
-    xs[1].send_own_down()
-    act[1].take_pair_far()
-    act[0].take_pair_down()
-    loads[4].wait()
-    w1t[...] = w1[...].T
-    act[1].give_mate()
+    act[2].give_mate()
+    second_grad(0, 0)
+    second_grad(1, 0)
+    xs[0].take_other_up()
     hid[2].cross()
-    pre[0].take(1)
-    xs[0].take_other_up()
-    pre[0].take(4)
+    xs[0].take_up()
+    pre[0].take(3)
+    xs[1].send_other_up()
+    act[1].send_pair_far()
+    xs[1].take_other_down()
+    xs[1].send_far_down()
+    pre[0].take(5)
+    pre[0].take(6)
+    act[3].take_pair_down()
+    xs[0].take_other_down()
+    act[1].take_pair_down()
+    act[3].send_pair_far()
     pre[1].take(0)
-    pre[1].take(1)
-    pre_grad(2)
-    pre[2].start()
-    pre[0].take(3)
-    act[1].take_mate()
+    xs[1].take_other_up()
     xs[0].send_far_down()
-    act[0].send_pair_up()
-    act[0].send_pair_far()
-    second_grad(0, 1)
-    pre[0].take(6)
-    pre[0].take(5)
-    second_grad(1, 1)
-    xs[1].take_other_up()
-    pre[1].take(4)
-    pre[1].take(2)
-    pre[2].take(0)
-    pre[1].take(3)
+    xs[0].send_far_up()
     pre[0].take_mate()
     input_part(0, 2)
     dx[0].far()
+    pre_grad(2)
+    pre[2].start()
+    pre[1].take(2)
     input_part(0, 1, 3, 0)
     dx[0].near()
+    act[1].take_pair_far()
+    pre[1].take(1)
+    pre[1].take(4)
+    xs[1].take_far_up()
+    xs[1].take_far_down()
+    xs[0].send_own_down()
+    act[3].take_pair_up()
+    act[2].send_own_pair()
+    xs[0].take_far_down()
+    act[3].take_pair()
+    act[1].take_mate()
+    second_grad(1, 1)
+    act[3].take_pair_far()
+    dx[0].fold(1)
+    pre[1].take(3)
+    act[2].send_pair_up()
+    pre[2].take(0)
+    pre[2].take(1)
+    act[2].send_half_up()
     pre[2].take(2)
-    xs[0].take_far_down()
+    second_grad(0, 1)
+    dx[0].fold(0)
+    act[3].take_mate()
+    xs[0].take_far_up()
+    pre[1].take(6)
+    act[2].send_pair_down()
+    act[2].send_half_down()
+    pre[1].take(5)
     xs[0].take_down()
-    pre[1].take(5)
-    pre[1].take(6)
-    dx[0].fold(0)
-    act[0].take_pair_up()
-    dx[0].fold(1)
-    xs[1].take_up()
-    xs[0].take_far_up()
+    second_grad(1, 3)
+    act[2].take_pair()
+    pre[2].take(4)
+    dx[0].cross()
     xs[1].take_down()
-    pre[2].take(1)
-    xs[1].send_far_up()
+    act[2].take_pair_up()
     pre[1].take_mate()
-    pre[2].take(4)
     input_part(1, 2)
     dx[1].far()
-    act[0].take_pair_far()
+    pre[2].take(3)
+    act[2].take_pair_down()
     input_part(1, 1, 3, 0)
     dx[1].near()
-    act[0].take_mate()
-    pre[2].take(3)
     pre[2].take(5)
-    dx[0].cross()
+    input_grad(0)
     pre[2].take(6)
+    second_grad(0, 3)
+    act[2].take_far()
+    act[2].send_pair_far()
+    dx[1].fold(0)
     dx[1].fold(1)
-    second_grad(0, 0)
     pre[2].take_mate()
-    loads[3].wait()
     input_part(2, 2)
-    dx[2].far()
+    dx[2].direct(2)
     input_part(2, 1, 3, 0)
-    dx[2].near()
-    xs[1].take_far_up()
+    dx[2].direct(1, 3, 0)
+    first_grad(3)
+    dx[1].cross()
+    act[2].take_pair_far()
     first_grad(0)
-    dx[1].fold(0)
-    dx[2].fold(1)
-    dx[1].cross()
-    second_grad(1, 0)
+    first_grad(2)
+    act[2].take_mate()
+    second_grad(0, 2)
+    second_grad(1, 2)
     first_grad(1)
-    dx[2].fold(0)
-    dx[2].cross()
-    input_grad(0)
-    first_grad(3)
-    first_grad(2)
+    input_grad(2, True)
     input_grad(1)
-    input_grad(2)
     for item in (*og, *xs, *act, *pre, *hid, *dx):
         item.drain()
     for copy in to_mate:
@@ -577,7 +688,7 @@
             vm(7, T, W),
             vm(2 * U, W),
             vm(2, W, U),
-            sem((S, 16)), sem((S, 16)), sem((X, 7)), sem((X, 7)), sem((F, 16)), sem((F, 16)), sem((S, 16)), sem((S, 16)),
+            sem((S, 16)), sem((S, 16)), sem((X, 7)), sem((X, 7)), sem((F, 18)), sem((F, 18)), sem((S, 16)), sem((S, 16)),
             sem((S, 7)), sem((S, 7)), sem((S, 7)), sem((S, 7)), sem((2,)), sem((2,)), sem((5,)),
         ],
         compiler_params=pltpu.CompilerParams(

time: 98.3 us -> 96.4 us (0.981); the launches traced: 97 us -> 96.3 us
  no operation moved by 1% of the time
where the time goes in v4:
time: 96.4 us; the launch traced here: 96.3 us
  Pallas kernels  95.5 us (99%)
    pallas_call x1, Pallas kernels, local(): pl.pallas_call(kernel, out_shape=(pltpu.VMEM((T, W), BF), pltpu.VMEM((W,...  91.7 us
    pallas_call x1, Pallas kernels, local(): pl.pallas_call(write_out, out_shape=[jax.ShapeDtypeStruct(array.shape, BF...  3.77 us

profile of v4, /device:TPU:1, one launch (start us, length us, event | category | flops | bytes accessed | tf_op | source)
XLA Modules:
  0.0 96.3 jit_solution(11048166558142317381)
XLA Ops:
  0.6 91.7 %ffn_back.1 = (bf16[128,768]{1,0:T(8,128)(2,1)S(1)}, bf16[768,3072]{1,0:T(8,128)(2,1)S(1)}, bf16[3072,768]{1,0:T(8,128)(2,1)S(1)}) custom-call(bf16[128,768]{1,0:T(8,128)(2,1)} %in_ref.1, bf16[64,3072]{1,0:T(8,128)(2,1)} %pre_ref.1, bf16[768,3072]{1,0:T(8,128)(2,1)} %w1_ref.1, bf16[3072,768]{1,0:T(8,128)(2,1)} %w2_ref.1, bf16[128,768]{1,0:T(8,128)(2,1)} %og_ref.1), custom_call_target="tpu_custom_call" | custom-call | flops 19327352832 | bytes 20000000 | tf_op jit(solution)/shard_map/ffn_back/pallas_call | solution.py:667
  92.3 3.8 %write_out.1 = (bf16[128,768]{1,0:T(8,128)(2,1)}, bf16[768,3072]{1,0:T(8,128)(2,1)}, bf16[3072,768]{1,0:T(8,128)(2,1)}) custom-call(bf16[128,768]{1,0:T(8,128)(2,1)S(1)} %get-tuple-element.6.dx, bf16[768,3072]{1,0:T(8,128)(2,1)S(1)} %get-tuple-element.7.dw1, bf16[3072,768]{1,0:T(8,128)(2,1)S(1)} %get-tuple-element.8.dw2), custom_call_target="tpu_custom_call" | custom-call | tf_op jit(solution)/shard_map/write_out/pallas_call | solution.py:700

commit v5 on v4

--- a/solution.py
+++ b/solution.py
@@ -642,19 +642,21 @@
     second_grad(0, 2)
     second_grad(1, 2)
     first_grad(1)
-    input_grad(2, True)
     input_grad(1)
-    for item in (*og, *xs, *act, *pre, *hid, *dx):
+    for item in (*og, *xs, *act, *pre, *hid, *dx[:-1]):
         item.drain()
     for copy in to_mate:
         copy.wait_send()
+    input_grad(2, True)
+    dx[-1].drain()
 
 
 def write_out(dx, dw1, dw2, dx_out, dw1_out, dw2_out, sems):
-    copies = [
-        pltpu.make_async_copy(src, dst, sems.at[i])
-        for i, (src, dst) in enumerate(((dw1, dw1_out), (dw2, dw2_out), (dx, dx_out)))
-    ]
+    copies = []
+    for src, dst in ((dw1, dw1_out), (dw2, dw2_out), (dx, dx_out)):
+        rows = src.shape[0] // 4
+        for at in (pl.ds(n * rows, rows) for n in range(4)):
+            copies.append(pltpu.make_async_copy(src.at[at], dst.at[at], sems.at[len(copies)]))
     for copy in copies:
         copy.start()
     for copy in copies:
@@ -702,7 +704,7 @@
         out_shape=[jax.ShapeDtypeStruct(array.shape, BF) for array in results],
         in_specs=[pl.BlockSpec(memory_space=pltpu.VMEM)] * 3,
         out_specs=[pl.BlockSpec(memory_space=pl.ANY)] * 3,
-        scratch_shapes=[sem((3,))],
+        scratch_shapes=[sem((12,))],
         compiler_params=pltpu.CompilerParams(vmem_limit_bytes=1024 * 1024),
         name="write_out",
     )(*results)

time: 96.4 us -> 96.4 us (level)
  no operation moved by 1% of the time
where the time goes in v5:
time: 96.4 us; the launch traced here: 96.2 us
  Pallas kernels  95.4 us (99%)
    pallas_call x1, Pallas kernels, local(): pl.pallas_call(kernel, out_shape=(pltpu.VMEM((T, W), BF), pltpu.VMEM((W,...  91.7 us
    pallas_call x1, Pallas kernels, local(): pl.pallas_call(write_out, out_shape=[jax.ShapeDtypeStruct(array.shape, BF...  3.75 us

profile of v5, /device:TPU:1, one launch (start us, length us, event | category | flops | bytes accessed | tf_op | source)
XLA Modules:
  0.0 96.2 jit_solution(15953853150852955896)
XLA Ops:
  0.6 91.7 %ffn_back.1 = (bf16[128,768]{1,0:T(8,128)(2,1)S(1)}, bf16[768,3072]{1,0:T(8,128)(2,1)S(1)}, bf16[3072,768]{1,0:T(8,128)(2,1)S(1)}) custom-call(bf16[128,768]{1,0:T(8,128)(2,1)} %in_ref.1, bf16[64,3072]{1,0:T(8,128)(2,1)} %pre_ref.1, bf16[768,3072]{1,0:T(8,128)(2,1)} %w1_ref.1, bf16[3072,768]{1,0:T(8,128)(2,1)} %w2_ref.1, bf16[128,768]{1,0:T(8,128)(2,1)} %og_ref.1), custom_call_target="tpu_custom_call" | custom-call | flops 19327352832 | bytes 20000000 | tf_op jit(solution)/shard_map/ffn_back/pallas_call | solution.py:669
  92.3 3.7 %write_out.1 = (bf16[128,768]{1,0:T(8,128)(2,1)}, bf16[768,3072]{1,0:T(8,128)(2,1)}, bf16[3072,768]{1,0:T(8,128)(2,1)}) custom-call(bf16[128,768]{1,0:T(8,128)(2,1)S(1)} %get-tuple-element.6.dx, bf16[768,3072]{1,0:T(8,128)(2,1)S(1)} %get-tuple-element.7.dw1, bf16[3072,768]{1,0:T(8,128)(2,1)S(1)} %get-tuple-element.8.dw2), custom_call_target="tpu_custom_call" | custom-call | tf_op jit(solution)/shard_map/write_out/pallas_call | solution.py:702
